TPU v7x, 32 devices: a whole 2x2x4 slice. The times are simulated.
32 devices in a mesh: grp: 2 (over x), sp: 16 (over z, y, core).
Axes of the slice: x: 2, y: 2, z: 4, core: 2. Of those that a mesh axis runs over, the one named last changes fastest.
Arguments:
- tokens: bfloat16 [2, 6, 1024, 1152], P('grp', None, 'sp'), parts along dimension 0, may hold values from -6 to 6
- gain_spatial: float32 [1152], replicated, may hold values from 0.5 to 1.5
- qkv_spatial: bfloat16 [1152, 1728], replicated, may hold values from -0.25 to 0.25
- out_spatial: bfloat16 [576, 1152], replicated, may hold values from -0.75 to 0.75
- gain_cross: float32 [1152], replicated, may hold values from 0.5 to 1.5
- qkv_cross: bfloat16 [1152, 1728], replicated, may hold values from -0.25 to 0.25
- out_cross: bfloat16 [576, 1152], replicated, may hold values from -0.75 to 0.75
- lengths: int32 [2, 6], P('grp'), parts along dimension 0, may hold values from 512 to 1024, as said below
- left_view: int32 [2, 6], P('grp'), parts along dimension 0, may hold values from 0 to 5, as said below
- right_view: int32 [2, 6], P('grp'), parts along dimension 0, may hold values from 0 to 5, as said below
- window_mask: int32 [2, 6, 8, 8], P('grp'), parts along dimension 0, may hold values from 0 to 1, as said below
Outputs:
- result: bfloat16 [2, 6, 1024, 1152], P('grp', None, 'sp'), parts along dimension 0
There are 2 independent parts, one for each index of `grp`. A program takes and returns all parts, laid end to end along the dimension named above; an argument that names none is the same for every part. Nothing has to cross between parts.
Inputs may be any that keep to these rules, and one draw needn't show every extreme that they name: `lengths`: in every frame some view has exactly 1024 live tokens. In each frame the views form one cycle: right_view[f, left_view[f, v]] = v, and no view is its own neighbour. In each frame the views form one cycle: left_view[f, right_view[f, v]] = v, and no view is its own neighbour. window_mask[f, v, a, b] is 1 where b = a or b = 0, and 0 where b > 0 and the distance of a and b exceeds 2.
All inputs are finite; a program needn't handle non-finite values.
Results may differ from a plain program's by a relative error of at most 0.035.
The roundings to bfloat16 on the way count: a program that leaves them out, or rounds other values in their place, can miss the bound.
Values may be sent and summed in bfloat16 or wider, within the bound.
No kernel may reach another device: no remote copies, remote signals or barrier semaphores. Data moves between devices by JAX's collectives and lax.ppermute only.
A program may use at most 128 MiB of HBM per device.

v0:
```python
import functools

import jax
import jax.numpy as jnp
from jax import lax
from jax.experimental import pallas as pl
from jax.experimental.pallas import tpu as pltpu
from jax.sharding import PartitionSpec as P

HEADS = 8
EPSILON = 1e-06


HS = 72
TILE = 64
LANES = 128
TOP = 40
QKV_ROWS = 336
OUT_ROWS = 112
NEG = -1e30
VMEM = 56 * 1024 * 1024


def cycle_order(right_ref):
    order = [jnp.int32(0)]
    for _ in range(5):
        order.append(right_ref[0, order[-1]])
    return order


def low_lanes(rows):
    return lax.broadcasted_iota(jnp.int32, (rows, LANES), 1) < TILE


def swap(tile):
    return pltpu.roll(tile, TILE, 1)


def side_by_side(first, first_half, second, second_half):
    left = first if first_half == 0 else swap(first)
    right = second if second_half == 1 else swap(second)
    return jnp.where(low_lanes(first.shape[0]), left, right)


def fold_third(tile, half):
    bottom = jnp.concatenate([tile[TOP:], jnp.zeros((2 * TOP - HS, LANES), jnp.float32)], axis=0)
    return side_by_side(tile[:TOP], half, bottom, half)


def normalise(floats, gain):
    square = jnp.mean(floats * floats, axis=-1, keepdims=True)
    return (floats * lax.rsqrt(square + EPSILON) * gain).astype(jnp.bfloat16)


def project_and_pack(normed_ref, weight_ref, turned_ref, out_ref, cross):
    total = weight_ref.shape[1]
    inner = total // 3
    step = 384
    for start in range(0, total, step):
        stop = min(start + step, total)
        part = jnp.dot(
            normed_ref[...], weight_ref[:, start:stop], preferred_element_type=jnp.float32
        )
        turned_ref[start:stop, :] = part.T
    for head in range(HEADS):
        for parity in range(2):
            other = 1 - parity if cross else parity

            def item(which, m):
                row = which * inner + head * HS
                return turned_ref[row : row + HS, m * LANES : (m + 1) * LANES]

            rows = [
                side_by_side(item(0, m), parity, item(1, m), other) for m in range(3)
            ]
            rows.append(side_by_side(item(2, 0), other, item(2, 1), other))
            rows.append(fold_third(item(2, 2), other))
            rows.append(jnp.zeros((QKV_ROWS - 4 * HS - TOP, LANES), jnp.float32))
            out_ref[head * 2 + parity] = jnp.concatenate(rows, axis=0).astype(jnp.bfloat16)


def project_kernel(right_ref, tokens_ref, gain_ref, weight_ref, out_ref, normed_ref, turned_ref):
    order = cycle_order(right_ref)
    for j in range(6):
        floats = tokens_ref[0, order[j]].astype(jnp.float32)
        normed_ref[j * TILE : (j + 1) * TILE, :] = normalise(floats, gain_ref[...])
    project_and_pack(normed_ref, weight_ref, turned_ref, out_ref, False)


def unpack(slots_ref, key_bias, query_rows, query_ref, key_ref, value_ref):
    blocks = slots_ref.shape[0] // 2
    low = low_lanes(QKV_ROWS)
    row8 = lax.broadcasted_iota(jnp.int32, (8, LANES), 0)
    pad = jnp.zeros((LANES - HS - 16, LANES), jnp.float32)
    first_row = jnp.where(row8 == 0, 1.0, 0.0)
    for b in range(blocks):
        span = slice(b * LANES, (b + 1) * LANES)
        even = slots_ref[2 * b].astype(jnp.float32)
        odd = slots_ref[2 * b + 1].astype(jnp.float32)
        lower = jnp.where(low, even, swap(odd))
        upper = jnp.where(low, swap(even), odd)
        own_block = jnp.where(row8 == b, 1.0, 0.0)
        values = [
            lower[3 * HS : 4 * HS],
            upper[3 * HS : 4 * HS],
            jnp.concatenate(
                [lower[4 * HS : 4 * HS + TOP], upper[4 * HS : 5 * HS - TOP]], axis=0
            ),
        ]
        for m in range(3):
            query = jnp.concatenate(
                [lower[m * HS : (m + 1) * HS], query_rows(m, b, row8), first_row, pad], axis=0
            )
            query_ref[m, :, span] = query.astype(jnp.bfloat16)
            live = jnp.where(row8 == 0, key_bias(m, b), 0.0)
            key = jnp.concatenate([upper[m * HS : (m + 1) * HS], own_block, live, pad], axis=0)
            key_ref[m, span, :] = key.T.astype(jnp.bfloat16)
            value_ref[m, :, span] = jnp.concatenate([values[m], first_row], axis=0).astype(
                jnp.bfloat16
            )


def attend(query, parts):
    factor = HS**-0.5 * 1.4426950408889634
    scores = [jnp.dot(keys, query, preferred_element_type=jnp.float32) for keys, _ in parts]
    top = functools.reduce(
        jnp.maximum, [jnp.max(score, axis=0, keepdims=True) for score in scores]
    )
    total = None
    for score, (_, values) in zip(scores, parts):
        weights = jnp.exp2((score - top) * factor).astype(jnp.bfloat16)
        term = jnp.dot(values, weights, preferred_element_type=jnp.float32)
        total = term if total is None else total + term
    return total[:HS] / total[HS : HS + 1]


def pack_outputs(attended_ref, out_ref):
    for b in range(out_ref.shape[0] // 2):
        span = slice(b * LANES, (b + 1) * LANES)
        tiles = [attended_ref[m, :, span] for m in range(3)]
        for half in range(2):
            rows = [side_by_side(tiles[0], half, tiles[1], half), fold_third(tiles[2], half)]
            out_ref[2 * b + half] = jnp.concatenate(rows, axis=0).astype(jnp.bfloat16)


def live_bias(length, b):
    position = b * LANES + lax.broadcasted_iota(jnp.int32, (8, LANES), 1)
    return jnp.where(position < length, 0.0, NEG)


def spatial_kernel(
    device_ref,
    right_ref,
    lengths_ref,
    mask_ref,
    slots_ref,
    out_ref,
    query_ref,
    key_ref,
    value_ref,
    attended_ref,
):
    order = cycle_order(right_ref)
    parity = device_ref[0] % 2
    views = [jnp.where(parity == 0, order[2 * m], order[2 * m + 1]) for m in range(3)]
    blocks = mask_ref.shape[-1]

    def query_rows(m, b, row8):
        rows = jnp.zeros((8, LANES), jnp.float32)
        for other in range(blocks):
            allowed = mask_ref[0, views[m], b, other] > 0
            rows = jnp.where(row8 == other, jnp.where(allowed, 0.0, NEG), rows)
        return rows

    def key_bias(m, b):
        return live_bias(lengths_ref[0, views[m]], b)

    unpack(slots_ref, key_bias, query_rows, query_ref, key_ref, value_ref)
    wide = 2 * LANES
    for m in range(3):
        for i in range(blocks // 2):
            first = max(0, 2 * i - 2) * LANES
            last = min(blocks, 2 * i + 4) * LANES
            spans = [slice(first, last)]
            if first > 0:
                spans.append(slice(0, LANES))
            lanes = slice(i * wide, (i + 1) * wide)
            attended_ref[m, :, lanes] = attend(
                query_ref[m, :, lanes],
                [(key_ref[m, span, :], value_ref[m, :, span]) for span in spans],
            )
    pack_outputs(attended_ref, out_ref)


def cross_kernel(
    device_ref,
    right_ref,
    lengths_ref,
    slots_ref,
    out_ref,
    query_ref,
    key_ref,
    value_ref,
    attended_ref,
):
    order = cycle_order(right_ref)
    parity = device_ref[0] % 2
    views = [jnp.where(parity == 0, order[2 * m + 1], order[2 * m]) for m in range(3)]

    def query_rows(m, b, row8):
        return jnp.zeros((8, LANES), jnp.float32)

    def key_bias(m, b):
        return live_bias(lengths_ref[0, views[m]], b)

    unpack(slots_ref, key_bias, query_rows, query_ref, key_ref, value_ref)
    wide = 2 * LANES
    for m in range(3):
        second = jnp.where(parity == 0, (m + 2) % 3, (m + 1) % 3)
        for i in range(query_ref.shape[2] // wide):
            lanes = slice(i * wide, (i + 1) * wide)
            attended_ref[m, :, lanes] = attend(
                query_ref[m, :, lanes],
                [(key_ref[m], value_ref[m]), (key_ref[second], value_ref[second])],
            )
    pack_outputs(attended_ref, out_ref)


def merge_heads(slots_ref, merged_ref):
    low = low_lanes(OUT_ROWS)
    tiles = [[], [], []]
    for head in range(HEADS):
        even = slots_ref[2 * head].astype(jnp.float32)
        odd = slots_ref[2 * head + 1].astype(jnp.float32)
        lower = jnp.where(low, even, swap(odd))
        upper = jnp.where(low, swap(even), odd)
        tiles[0].append(lower[:HS])
        tiles[1].append(upper[:HS])
        tiles[2].append(lower[HS:])
        tiles[2].append(upper[HS : 2 * HS - TOP])
    for m in range(3):
        merged = jnp.concatenate(tiles[m], axis=0)
        merged_ref[m * LANES : (m + 1) * LANES, :] = merged.T.astype(jnp.bfloat16)


def live_rows(device_ref, length):
    position = device_ref[0] * TILE + lax.broadcasted_iota(jnp.int32, (TILE, 1), 0)
    return (position < length).astype(jnp.float32)


def middle_kernel(
    device_ref,
    right_ref,
    lengths_ref,
    slots_ref,
    tokens_ref,
    mix_ref,
    gain_ref,
    weight_ref,
    middle_ref,
    out_ref,
    merged_ref,
    normed_ref,
    turned_ref,
):
    order = cycle_order(right_ref)
    merge_heads(slots_ref, merged_ref)
    for j in range(6):
        rows = slice(j * TILE, (j + 1) * TILE)
        branch = jnp.dot(merged_ref[rows, :], mix_ref[...], preferred_element_type=jnp.float32)
        live = live_rows(device_ref, lengths_ref[0, order[j]])
        middle = (tokens_ref[0, order[j]].astype(jnp.float32) + live * branch).astype(jnp.bfloat16)
        middle_ref[rows, :] = middle
        normed_ref[rows, :] = normalise(middle.astype(jnp.float32), gain_ref[...])
    project_and_pack(normed_ref, weight_ref, turned_ref, out_ref, True)


def finish_kernel(
    device_ref, right_ref, lengths_ref, slots_ref, middle_ref, mix_ref, out_ref, merged_ref
):
    order = cycle_order(right_ref)
    merge_heads(slots_ref, merged_ref)
    for j in range(6):
        rows = slice(j * TILE, (j + 1) * TILE)
        branch = jnp.dot(merged_ref[rows, :], mix_ref[...], preferred_element_type=jnp.float32)
        live = live_rows(device_ref, lengths_ref[0, order[j]])
        out_ref[0, order[j]] = (middle_ref[rows, :].astype(jnp.float32) + live * branch).astype(
            jnp.bfloat16
        )


def call(kernel, scalars, arrays, out_shape, scratch, name):
    smem = pl.BlockSpec(memory_space=pltpu.SMEM)
    vmem = pl.BlockSpec(memory_space=pltpu.VMEM)
    return pl.pallas_call(
        kernel,
        out_shape=out_shape,
        in_specs=[smem] * len(scalars) + [vmem] * len(arrays),
        out_specs=jax.tree.map(lambda _: vmem, out_shape),
        scratch_shapes=scratch,
        compiler_params=pltpu.CompilerParams(vmem_limit_bytes=VMEM),
        name=name,
    )(*scalars, *arrays)


def exchange(slots):
    return lax.all_to_all(slots, "sp", split_axis=0, concat_axis=0, tiled=True)


def fast_shards(
    tokens,
    gain_spatial,
    qkv_spatial,
    out_spatial,
    gain_cross,
    qkv_cross,
    out_cross,
    lengths,
    left_view,
    right_view,
    window_mask,
):
    width = tokens.shape[-1]
    inner = out_spatial.shape[0]
    devices_sp = lax.axis_size("sp")
    view_len = TILE * devices_sp
    rows = 6 * TILE
    device = lax.axis_index("sp").astype(jnp.int32).reshape(1)
    qkv_slots = jax.ShapeDtypeStruct((devices_sp, QKV_ROWS, LANES), jnp.bfloat16)
    out_slots = jax.ShapeDtypeStruct((devices_sp, OUT_ROWS, LANES), jnp.bfloat16)
    turned = pltpu.VMEM((3 * inner, rows), jnp.float32)
    normed = pltpu.VMEM((rows, width), jnp.bfloat16)
    merged = pltpu.VMEM((rows, inner), jnp.bfloat16)
    heads = [
        pltpu.VMEM((3, LANES, view_len), jnp.bfloat16),
        pltpu.VMEM((3, view_len, LANES), jnp.bfloat16),
        pltpu.VMEM((3, HS + 8, view_len), jnp.bfloat16),
        pltpu.VMEM((3, HS, view_len), jnp.float32),
    ]
    slots = call(
        project_kernel,
        [right_view],
        [tokens, gain_spatial.reshape(1, width), qkv_spatial],
        qkv_slots,
        [normed, turned],
        "project",
    )
    attended = call(
        spatial_kernel,
        [device, right_view, lengths, window_mask],
        [exchange(slots)],
        out_slots,
        heads,
        "spatial",
    )
    middle, slots = call(
        middle_kernel,
        [device, right_view, lengths],
        [exchange(attended), tokens, out_spatial, gain_cross.reshape(1, width), qkv_cross],
        (jax.ShapeDtypeStruct((rows, width), jnp.bfloat16), qkv_slots),
        [merged, normed, turned],
        "middle",
    )
    attended = call(
        cross_kernel,
        [device, right_view, lengths],
        [exchange(slots)],
        out_slots,
        heads,
        "cross",
    )
    return call(
        finish_kernel,
        [device, right_view, lengths],
        [exchange(attended), middle, out_cross],
        jax.ShapeDtypeStruct(tokens.shape, jnp.bfloat16),
        [merged],
        "finish",
    )


def rms_norm(values, gain):
    floats = values.astype(jnp.float32)
    square = jnp.mean(floats * floats, axis=-1, keepdims=True)
    return (floats * lax.rsqrt(square + EPSILON) * gain).astype(jnp.bfloat16)


def to_frames(block, heads):
    frames, views, tile_len, inner = block.shape
    head_size = inner // heads
    moved = block.reshape(frames, views, tile_len, heads, head_size).transpose(0, 3, 1, 2, 4)
    return moved.reshape(frames, heads, views, tile_len * head_size)


def from_units(units, frames, views, tile_len, heads):
    head_size = units.shape[-1] // tile_len
    moved = units.reshape(frames, heads, views, tile_len, head_size).transpose(0, 2, 3, 1, 4)
    return moved.reshape(frames, views, tile_len, heads * head_size)


def attend_one(operands):
    query, keys, values, allow = operands
    scores = jnp.einsum("qd,kd->qk", query, keys, preferred_element_type=jnp.float32) * query.shape[
        -1
    ] ** (-0.5)
    scores = jnp.where(allow, scores, -1e30)
    top = jnp.max(scores, axis=-1, keepdims=True)
    weights = jnp.where(allow, jnp.exp(scores - top), 0.0)
    probs = (weights / jnp.sum(weights, axis=-1, keepdims=True)).astype(jnp.bfloat16)
    return jnp.einsum("qk,kd->qd", probs, values, preferred_element_type=jnp.float32).astype(
        jnp.bfloat16
    )


def general_shards(
    tokens,
    gain_spatial,
    qkv_spatial,
    out_spatial,
    gain_cross,
    qkv_cross,
    out_cross,
    lengths,
    left_view,
    right_view,
    window_mask,
):
    frames, views, tile_len, width = tokens.shape
    inner = out_spatial.shape[0]
    head_size = inner // HEADS
    devices_sp = lax.axis_size("sp")
    device = lax.axis_index("sp")
    view_len = tile_len * devices_sp
    blocks = window_mask.shape[-1]
    block_len = view_len // blocks
    positions = device * tile_len + jnp.arange(tile_len, dtype=jnp.int32)
    live_rows = (positions[None, None, :] < lengths[:, :, None]).astype(jnp.float32)[..., None]
    key_pos = jnp.arange(view_len, dtype=jnp.int32)
    units_dev = frames * HEADS * views // devices_sp
    unit_ids = device * units_dev + jnp.arange(units_dev, dtype=jnp.int32)
    frame_ids = unit_ids // (HEADS * views)
    view_ids = unit_ids % views
    flat_ids = frame_ids * views + view_ids
    flat_len = lengths.reshape(-1)
    own_len = jnp.take(flat_len, flat_ids)
    total_units = frames * HEADS * views
    normed = rms_norm(tokens, gain_spatial)
    projected = jnp.einsum(
        "fvtd,de->fvte", normed, qkv_spatial, preferred_element_type=jnp.float32
    ).astype(jnp.bfloat16)
    stacked = jnp.stack(
        [
            to_frames(projected[..., which * inner : (which + 1) * inner], HEADS)
            for which in range(3)
        ],
        axis=3,
    )
    stacked = stacked.reshape(total_units, 3, tile_len * head_size)
    gathered = lax.all_to_all(stacked, "sp", split_axis=0, concat_axis=2, tiled=True)
    gathered = gathered.reshape(units_dev, 3, view_len, head_size)
    masks = jnp.take(window_mask.reshape(-1, blocks, blocks), flat_ids, axis=0) > 0
    allow = jnp.broadcast_to(
        masks[:, :, None, :, None], (units_dev, blocks, block_len, blocks, block_len)
    )
    allow = allow.reshape(units_dev, view_len, view_len) & (
        key_pos[None, None, :] < own_len[:, None, None]
    )
    spatial_out = lax.map(attend_one, (gathered[:, 0], gathered[:, 1], gathered[:, 2], allow))
    returned = lax.all_to_all(
        spatial_out.reshape(units_dev, view_len * head_size),
        "sp",
        split_axis=1,
        concat_axis=0,
        tiled=True,
    )
    attended = from_units(returned, frames, views, tile_len, HEADS)
    branch = jnp.einsum("fvte,ed->fvtd", attended, out_spatial, preferred_element_type=jnp.float32)
    middle = (tokens.astype(jnp.float32) + live_rows * branch).astype(jnp.bfloat16)
    normed_cross = rms_norm(middle, gain_cross)
    projected = jnp.einsum(
        "fvtd,de->fvte", normed_cross, qkv_cross, preferred_element_type=jnp.float32
    ).astype(jnp.bfloat16)
    query_fr, key_fr, value_fr = [
        to_frames(projected[..., which * inner : (which + 1) * inner], HEADS) for which in range(3)
    ]
    left_ids = jnp.take(left_view.reshape(-1), flat_ids)
    right_ids = jnp.take(right_view.reshape(-1), flat_ids)
    view_iota = jnp.arange(views, dtype=jnp.int32)
    pick_left = (left_view[:, :, None] == view_iota).astype(jnp.bfloat16)
    pick_right = (right_view[:, :, None] == view_iota).astype(jnp.bfloat16)

    def select(pick, source):
        return jnp.einsum(
            "fvw,fhwx->fhvx", pick, source, preferred_element_type=jnp.float32
        ).astype(jnp.bfloat16)

    packed = jnp.stack(
        [
            query_fr,
            select(pick_left, key_fr),
            select(pick_left, value_fr),
            select(pick_right, key_fr),
            select(pick_right, value_fr),
        ],
        axis=3,
    )
    packed = packed.reshape(total_units, 5, tile_len * head_size)
    arrived = lax.all_to_all(packed, "sp", split_axis=0, concat_axis=2, tiled=True)
    cross_query = arrived[:, 0]
    left_kv = arrived[:, 1:3]
    right_kv = arrived[:, 3:5]
    cross_keys = jnp.concatenate([left_kv[:, 0], right_kv[:, 0]], axis=1).reshape(
        units_dev, 2 * view_len, head_size
    )
    cross_values = jnp.concatenate([left_kv[:, 1], right_kv[:, 1]], axis=1).reshape(
        units_dev, 2 * view_len, head_size
    )
    left_len = jnp.take(flat_len, frame_ids * views + left_ids)
    right_len = jnp.take(flat_len, frame_ids * views + right_ids)
    allow_cross = jnp.concatenate(
        [key_pos[None, :] < left_len[:, None], key_pos[None, :] < right_len[:, None]], axis=1
    )[:, None, :]
    cross_out = lax.map(
        attend_one,
        (
            cross_query.reshape(units_dev, view_len, head_size),
            cross_keys,
            cross_values,
            allow_cross,
        ),
    )
    returned = lax.all_to_all(
        cross_out.reshape(units_dev, view_len * head_size),
        "sp",
        split_axis=1,
        concat_axis=0,
        tiled=True,
    )
    attended = from_units(returned, frames, views, tile_len, HEADS)
    branch = jnp.einsum("fvte,ed->fvtd", attended, out_cross, preferred_element_type=jnp.float32)
    return (middle.astype(jnp.float32) + live_rows * branch).astype(jnp.bfloat16)


def shards(*args):
    tokens, mask = args[0], args[-1]
    sizes = (tokens.shape[0], tokens.shape[1], tokens.shape[2], mask.shape[-1])
    if sizes == (1, 6, TILE, 8) and lax.axis_size("sp") == 2 * HEADS:
        return fast_shards(*args)
    return general_shards(*args)


def solution(mesh):
    in_specs = (
        P("grp", None, "sp", None),
        P(),
        P(),
        P(),
        P(),
        P(),
        P(),
        P("grp", None),
        P("grp", None),
        P("grp", None),
        P("grp", None, None, None),
    )
    out_specs = P("grp", None, "sp", None)
    return jax.shard_map(shards, mesh=mesh, in_specs=in_specs, out_specs=out_specs, check_vma=False)
```

profile of v0, /device:TPU:0, one launch (start us, length us, event | category | flops | bytes accessed | tf_op | source)
XLA Modules:
  0.0 164.8 jit_solution(18296970981792890905)
XLA Ops:
  0.0 1.3 reshape.10.gain_ref
  1.3 6.4 %copy.11.weight_ref = bf16[1152,1728]{1,0:T(8,128)(2,1)} copy(bf16[1152,1728]{0,1:T(8,128)(2,1)} %param.13) | data formatting | bytes 7962624 | tf_op args[2]
  7.7 6.7 %project.1 = bf16[16,336,128]{2,1,0:T(8,128)(2,1)} custom-call(s32[1,6]{1,0:T(1,128)} %right_ref.9, bf16[1,6,64,1152]{3,2,1,0:T(8,128)(2,1)} %tokens_ref.3, f32[1,1152]{1,0:T(1,128)} %reshape.10.gain_ref, bf16[1152,1728]{1,0:T(8,128)(2,1)} %copy.11.weight_ref), custom_call_target="tpu_custom_call" | custom-call | tf_op jit(solution)/shard_map/project/pallas_call | solution.py:295
  14.5 7.4 %all-to-all-start = ((bf16[16,336,128]{2,1,0:T(8,128)(2,1)}), bf16[16,336,128]{2,1,0:T(8,128)(2,1)S(1)}, u32[]{:S(2)}, u32[]{:S(2)}) async-start(bf16[16,336,128]{2,1,0:T(8,128)(2,1)} %project.1), calls=%async_computation | async-start | bytes 2752512 | tf_op jit(solution)/shard_map/all_to_all | solution.py:307
  21.8 28.6 %all-to-all-done.slots_ref = bf16[16,336,128]{2,1,0:T(8,128)(2,1)S(1)} async-done(((bf16[16,336,128]{2,1,0:T(8,128)(2,1)}), bf16[16,336,128]{2,1,0:T(8,128)(2,1)S(1)}, u32[]{:S(2)}, u32[]{:S(2)}) %all-to-all-start) | async-done | bytes 1376288 | tf_op jit(solution)/shard_map/all_to_all | solution.py:307
  50.4 0.0 copy-start
  50.4 1.1 copy-done
  51.5 0.0 copy-start.2
  51.5 8.5 %spatial.1 = bf16[16,112,128]{2,1,0:T(8,128)(2,1)} custom-call(s32[1]{0:T(128)} %bitcast.device_ref, s32[1,6]{1,0:T(1,128)} %right_ref.9, s32[1,6]{1,0:T(1,128)} %lengths_ref.7, s32[1,6,8,8]{3,2,1,0:T(8,128)} %mask_ref.1, bf16[16,336,128]{2,1,0:T(8,128)(2,1)} %copy-done), custom_call_target="tpu_custom_call" | custom-call | tf_op jit(solution)/shard_map/spatial/pallas_call | solution.py:295
  60.0 8.3 %all-to-all-start.1 = ((bf16[16,112,128]{2,1,0:T(8,128)(2,1)}), bf16[16,112,128]{2,1,0:T(8,128)(2,1)S(1)}, u32[]{:S(2)}, u32[]{:S(2)}) async-start(bf16[16,112,128]{2,1,0:T(8,128)(2,1)} %spatial.1), calls=%async_computation.1 | async-start | bytes 917504 | tf_op jit(solution)/shard_map/all_to_all | solution.py:307
  68.3 0.0 copy-done.2
  68.3 0.6 reshape.11.gain_ref
  68.9 6.4 %copy.12.weight_ref = bf16[1152,1728]{1,0:T(8,128)(2,1)} copy(bf16[1152,1728]{0,1:T(8,128)(2,1)} %param.16) | data formatting | bytes 7962624 | tf_op args[5]
  75.3 6.2 %all-to-all-done.1.slots_ref = bf16[16,112,128]{2,1,0:T(8,128)(2,1)S(1)} async-done(((bf16[16,112,128]{2,1,0:T(8,128)(2,1)}), bf16[16,112,128]{2,1,0:T(8,128)(2,1)S(1)}, u32[]{:S(2)}, u32[]{:S(2)}) %all-to-all-start.1) | async-done | bytes 458784 | tf_op jit(solution)/shard_map/all_to_all | solution.py:307
  81.5 0.0 copy-start.1
  81.5 0.8 copy-done.1
  82.3 8.8 %middle.1 = (bf16[384,1152]{1,0:T(8,128)(2,1)}, bf16[16,336,128]{2,1,0:T(8,128)(2,1)}) custom-call(s32[1]{0:T(128)} %bitcast.device_ref, s32[1,6]{1,0:T(1,128)} %right_ref.9, s32[1,6]{1,0:T(1,128)} %lengths_ref.7, bf16[16,112,128]{2,1,0:T(8,128)(2,1)} %copy-done.1, bf16[1,6,64,1152]{3,2,1,0:T(8,128)(2,1)} %tokens_ref.3, bf16[576,1152]{1,0:T(8,128)(2,1)} %mix_ref.2, ...), custom_call_target="tpu_custom_call" | custom-call | tf_op jit(solution)/shard_map/middle/pallas_call | solution.py:295
  91.0 37.0 %all_to_all.20.slots_ref = bf16[16,336,128]{2,1,0:T(8,128)(2,1)} all-to-all(bf16[16,336,128]{2,1,0:T(8,128)(2,1)} %get-tuple-element.7), channel_id=1, replica_groups=mesh['grp'=2,'sp'=16] {'sp'}, dimensions={0} | all-to-all | bytes 2752512 | tf_op jit(solution)/shard_map/all_to_all | solution.py:307
  128.1 15.0 %cross.1 = bf16[16,112,128]{2,1,0:T(8,128)(2,1)} custom-call(s32[1]{0:T(128)} %bitcast.device_ref, s32[1,6]{1,0:T(1,128)} %right_ref.9, s32[1,6]{1,0:T(1,128)} %lengths_ref.7, bf16[16,336,128]{2,1,0:T(8,128)(2,1)} %all_to_all.20.slots_ref), custom_call_target="tpu_custom_call" | custom-call | tf_op jit(solution)/shard_map/cross/pallas_call | solution.py:295
  143.0 17.5 %all_to_all.21.slots_ref = bf16[16,112,128]{2,1,0:T(8,128)(2,1)} all-to-all(bf16[16,112,128]{2,1,0:T(8,128)(2,1)} %cross.1), channel_id=1, replica_groups=mesh['grp'=2,'sp'=16] {'sp'}, dimensions={0} | all-to-all | bytes 917504 | tf_op jit(solution)/shard_map/all_to_all | solution.py:307
  160.5 4.3 %finish.1 = bf16[1,6,64,1152]{3,2,1,0:T(8,128)(2,1)} custom-call(s32[1]{0:T(128)} %bitcast.device_ref, s32[1,6]{1,0:T(1,128)} %right_ref.9, s32[1,6]{1,0:T(1,128)} %lengths_ref.7, bf16[16,112,128]{2,1,0:T(8,128)(2,1)} %all_to_all.21.slots_ref, bf16[384,1152]{1,0:T(8,128)(2,1)} %get-tuple-element.8.middle_ref, bf16[576,1152]{1,0:T(8,128)(2,1)} %mix_ref.3), custom_call_target="tpu_custom_call" | custom-call | tf_op jit(solution)/shard_map/finish/pallas_call | solution.py:295
Async XLA Ops:
  14.5 35.9 %all-to-all-start = ((bf16[16,336,128]{2,1,0:T(8,128)(2,1)}), bf16[16,336,128]{2,1,0:T(8,128)(2,1)S(1)}, u32[]{:S(2)}, u32[]{:S(2)}) async-start(bf16[16,336,128]{2,1,0:T(8,128)(2,1)} %project.1), calls=%async_computation | async-start | bytes 2752512 | tf_op jit(solution)/shard_map/all_to_all | solution.py:307
  50.4 1.1 copy-start
  51.5 16.8 %copy-start.2 = (f32[1152]{0:T(1024)S(1)}, f32[1152]{0:T(1024)}, u32[]{:S(2)}) copy-start(f32[1152]{0:T(1024)} %param.15) | copy-start | bytes 13828
  60.0 21.5 %all-to-all-start.1 = ((bf16[16,112,128]{2,1,0:T(8,128)(2,1)}), bf16[16,112,128]{2,1,0:T(8,128)(2,1)S(1)}, u32[]{:S(2)}, u32[]{:S(2)}) async-start(bf16[16,112,128]{2,1,0:T(8,128)(2,1)} %spatial.1), calls=%async_computation.1 | async-start | bytes 917504 | tf_op jit(solution)/shard_map/all_to_all | solution.py:307
  81.5 0.8 copy-start.1
where the time goes:
time: 166 us; the launch traced here: 165 us
  blocking collectives  54.5 us (33%)
  Pallas kernels  43.2 us (26%)
  waiting for transfers between devices  34.8 us (21%)
  local copies, waits for them, and re-layouts  16.6 us (10%)
  starting transfers between devices  15.7 us (9%)
    all_to_all x2, blocking collectives, exchange(): return lax.all_to_all(slots, 'sp', split_axis=0, concat_axis=0, tiled=True)  54.5 us
    pallas_call x5, Pallas kernels, call(): pl.pallas_call(kernel, out_shape=out_shape, in_specs=[smem] * len(scalars...  43.2 us
    all_to_all x2, waiting for transfers between devices, exchange(): return lax.all_to_all(slots, 'sp', split_axis=0, concat_axis=0, tiled=True)  34.8 us
    all_to_all x2, starting transfers between devices, exchange(): return lax.all_to_all(slots, 'sp', split_axis=0, concat_axis=0, tiled=True)  15.7 us
    unnamed x8, local copies, waits for them, and re-layouts  14.7 us
  transfers between devices with their start and end apart: 2, of which 2 were waited for; matrix products, arithmetic and copies ran while one was open for 4% of the time, Pallas kernels for 0%

commit v1 on v0

--- a/solution.py
+++ b/solution.py
@@ -18,7 +18,7 @@
 QKV_ROWS = 336
 OUT_ROWS = 112
 NEG = -1e30
-VMEM = 56 * 1024 * 1024
+VMEM = 24 * 1024 * 1024
 
 
 def cycle_order(right_ref):
@@ -49,19 +49,17 @@
 
 def normalise(floats, gain):
     square = jnp.mean(floats * floats, axis=-1, keepdims=True)
-    return (floats * lax.rsqrt(square + EPSILON) * gain).astype(jnp.bfloat16)
+    return (floats * lax.rsqrt(square + EPSILON) * gain[None, :]).astype(jnp.bfloat16)
 
 
 def project_and_pack(normed_ref, weight_ref, turned_ref, out_ref, cross):
-    total = weight_ref.shape[1]
-    inner = total // 3
-    step = 384
-    for start in range(0, total, step):
-        stop = min(start + step, total)
-        part = jnp.dot(
-            normed_ref[...], weight_ref[:, start:stop], preferred_element_type=jnp.float32
-        )
-        turned_ref[start:stop, :] = part.T
+    inner = weight_ref.shape[0] // 3
+    turned_ref[...] = lax.dot_general(
+        weight_ref[...],
+        normed_ref[...],
+        (((1,), (1,)), ((), ())),
+        preferred_element_type=jnp.float32,
+    )
     for head in range(HEADS):
         for parity in range(2):
             other = 1 - parity if cross else parity
@@ -340,7 +338,7 @@
     slots = call(
         project_kernel,
         [right_view],
-        [tokens, gain_spatial.reshape(1, width), qkv_spatial],
+        [tokens, gain_spatial, qkv_spatial.T],
         qkv_slots,
         [normed, turned],
         "project",
@@ -356,7 +354,7 @@
     middle, slots = call(
         middle_kernel,
         [device, right_view, lengths],
-        [exchange(attended), tokens, out_spatial, gain_cross.reshape(1, width), qkv_cross],
+        [exchange(attended), tokens, out_spatial, gain_cross, qkv_cross.T],
         (jax.ShapeDtypeStruct((rows, width), jnp.bfloat16), qkv_slots),
         [merged, normed, turned],
         "middle",

time: 166 us -> 152 us (0.916)
  blocking collectives: 54.5 us -> 75.2 us
  Pallas kernels: 43.2 us -> 33 us
  local copies, waits for them, and re-layouts: 16.6 us -> 6.8 us
  starting transfers between devices: 15.7 us -> 7.52 us
  waiting for transfers between devices: 34.8 us -> 28.6 us
    all_to_all x2 -> x3, blocking collectives: 54.5 us -> 75.2 us  [exchange(): return lax.all_to_all(slots, 'sp', split_axis=0, concat_axis=0, tiled=True)]
    pallas_call x5, Pallas kernels: 43.2 us -> 33 us  [call(): pl.pallas_call(kernel, out_shape=out_shape, in_specs=[smem] * len(scalars...]
    all_to_all x2 -> x1, starting transfers between devices: 15.7 us -> 7.52 us  [exchange(): return lax.all_to_all(slots, 'sp', split_axis=0, concat_axis=0, tiled=True)]
    unnamed x8 -> x24, local copies, waits for them, and re-layouts: 14.7 us -> 6.8 us
    all_to_all x2 -> x1, waiting for transfers between devices: 34.8 us -> 28.6 us  [exchange(): return lax.all_to_all(slots, 'sp', split_axis=0, concat_axis=0, tiled=True)]
    reshape x2 -> x0, local copies, waits for them, and re-layouts: 1.89 us -> none  [the longest x1 1.29 us: fast_shards(): gain_spatial.reshape(1, width)]
  transfers between devices with their start and end apart: 2 -> 1, of which waited for: 2 -> 1; matrix products, arithmetic and copies ran while one was open for 4% -> 0% of each run, Pallas kernels for 0% -> 0%
where the time goes in v1:
time: 152 us; the launch traced here: 151 us
  blocking collectives  75.2 us (49%)
  Pallas kernels  33 us (22%)
  waiting for transfers between devices  28.6 us (19%)
  starting transfers between devices  7.52 us (5%)
  local copies, waits for them, and re-layouts  6.8 us (4%)
    all_to_all x3, blocking collectives, exchange(): return lax.all_to_all(slots, 'sp', split_axis=0, concat_axis=0, tiled=True)  75.2 us
    pallas_call x5, Pallas kernels, call(): pl.pallas_call(kernel, out_shape=out_shape, in_specs=[smem] * len(scalars...  33 us
    all_to_all x1, waiting for transfers between devices, exchange(): return lax.all_to_all(slots, 'sp', split_axis=0, concat_axis=0, tiled=True)  28.6 us
    all_to_all x1, starting transfers between devices, exchange(): return lax.all_to_all(slots, 'sp', split_axis=0, concat_axis=0, tiled=True)  7.52 us
    unnamed x24, local copies, waits for them, and re-layouts  6.8 us
  transfers between devices with their start and end apart: 1, of which 1 were waited for; matrix products, arithmetic and copies ran while one was open for 0% of the time, Pallas kernels for 0%

profile of v1, /device:TPU:0, one launch (start us, length us, event | category | flops | bytes accessed | tf_op | source)
XLA Modules:
  0.0 151.1 jit_solution(13782096814662385867)
XLA Ops:
  0.0 2.1 %copy-done = bf16[1152,1728]{0,1:T(8,128)(2,1)S(1)} copy-done((bf16[1152,1728]{0,1:T(8,128)(2,1)S(1)}, bf16[1152,1728]{0,1:T(8,128)(2,1)}, u32[]{:S(2)}) %copy-start) | copy-done | bytes 3981336
  2.1 1.2 copy-done.2
  3.3 0.7 copy-done.7
  4.0 0.7 copy-done.9
  4.6 4.4 %project.1 = bf16[16,336,128]{2,1,0:T(8,128)(2,1)} custom-call(s32[1,6]{1,0:T(1,128)S(1)} %copy-done.7, bf16[1,6,64,1152]{3,2,1,0:T(8,128)(2,1)S(1)} %copy-done.2, f32[1152]{0:T(1024)S(1)} %copy-done.9, bf16[1728,1152]{1,0:T(8,128)(2,1)S(1)} %bitcast.3), custom_call_target="tpu_custom_call" | custom-call | tf_op jit(solution)/shard_map/project/pallas_call | solution.py:293
  9.1 7.5 %all-to-all-start = ((bf16[16,336,128]{2,1,0:T(8,128)(2,1)}), bf16[16,336,128]{2,1,0:T(8,128)(2,1)S(1)}, u32[]{:S(2)}, u32[]{:S(2)}) async-start(bf16[16,336,128]{2,1,0:T(8,128)(2,1)} %project.1), calls=%async_computation | async-start | bytes 2752512 | tf_op jit(solution)/shard_map/all_to_all | solution.py:305
  16.6 28.6 %all-to-all-done.slots_ref = bf16[16,336,128]{2,1,0:T(8,128)(2,1)S(1)} async-done(((bf16[16,336,128]{2,1,0:T(8,128)(2,1)}), bf16[16,336,128]{2,1,0:T(8,128)(2,1)S(1)}, u32[]{:S(2)}, u32[]{:S(2)}) %all-to-all-start) | async-done | bytes 1376288 | tf_op jit(solution)/shard_map/all_to_all | solution.py:305
  45.1 0.0 copy-done.6
  45.1 0.0 copy-done.8
  45.1 0.0 copy-done.11
  45.1 0.0 copy-start.3
  45.2 0.0 copy-start.4
  45.2 0.0 copy-start.10
  45.2 7.3 %spatial.1 = bf16[16,112,128]{2,1,0:T(8,128)(2,1)S(1)} custom-call(s32[1]{0:T(128)} %bitcast.device_ref, s32[1,6]{1,0:T(1,128)S(1)} %copy-done.8, s32[1,6]{1,0:T(1,128)S(1)} %copy-done.11, s32[1,6,8,8]{3,2,1,0:T(8,128)S(1)} %copy-done.6, bf16[16,336,128]{2,1,0:T(8,128)(2,1)S(1)} %all-to-all-done.slots_ref), custom_call_target="tpu_custom_call" | custom-call | tf_op jit(solution)/shard_map/spatial/pallas_call | solution.py:293
  52.5 21.3 %all_to_all.20.slots_ref = bf16[16,112,128]{2,1,0:T(8,128)(2,1)S(1)} all-to-all(bf16[16,112,128]{2,1,0:T(8,128)(2,1)S(1)} %spatial.1), channel_id=1, replica_groups=mesh['grp'=2,'sp'=16] {'sp'}, dimensions={0} | all-to-all | bytes 917504 | tf_op jit(solution)/shard_map/all_to_all | solution.py:305
  73.8 0.0 copy-done.3
  73.8 0.0 copy-done.10
  73.8 0.0 copy-start.1
  73.8 2.1 %copy-done.1 = bf16[1152,1728]{0,1:T(8,128)(2,1)S(1)} copy-done((bf16[1152,1728]{0,1:T(8,128)(2,1)S(1)}, bf16[1152,1728]{0,1:T(8,128)(2,1)}, u32[]{:S(2)}) %copy-start.1) | copy-done | bytes 3981336
  75.9 4.8 %middle.1 = (bf16[384,1152]{1,0:T(8,128)(2,1)S(1)}, bf16[16,336,128]{2,1,0:T(8,128)(2,1)S(1)}) custom-call(s32[1]{0:T(128)} %bitcast.device_ref, s32[1,6]{1,0:T(1,128)S(1)} %copy-done.8, s32[1,6]{1,0:T(1,128)S(1)} %copy-done.11, bf16[16,112,128]{2,1,0:T(8,128)(2,1)S(1)} %all_to_all.20.slots_ref, bf16[1,6,64,1152]{3,2,1,0:T(8,128)(2,1)S(1)} %copy-done.3, ...), custom_call_target="tpu_custom_call" | custom-call | tf_op jit(solution)/shard_map/middle/pallas_call | solution.py:293
  80.7 36.5 %all_to_all.21.slots_ref = bf16[16,336,128]{2,1,0:T(8,128)(2,1)S(1)} all-to-all(bf16[16,336,128]{2,1,0:T(8,128)(2,1)S(1)} %get-tuple-element.7), channel_id=1, replica_groups=mesh['grp'=2,'sp'=16] {'sp'}, dimensions={0} | all-to-all | bytes 2752512 | tf_op jit(solution)/shard_map/all_to_all | solution.py:305
  117.2 13.4 %cross.1 = bf16[16,112,128]{2,1,0:T(8,128)(2,1)S(1)} custom-call(s32[1]{0:T(128)} %bitcast.device_ref, s32[1,6]{1,0:T(1,128)S(1)} %copy-done.8, s32[1,6]{1,0:T(1,128)S(1)} %copy-done.11, bf16[16,336,128]{2,1,0:T(8,128)(2,1)S(1)} %all_to_all.21.slots_ref), custom_call_target="tpu_custom_call" | custom-call | tf_op jit(solution)/shard_map/cross/pallas_call | solution.py:293
  130.6 17.3 %all_to_all.22.slots_ref = bf16[16,112,128]{2,1,0:T(8,128)(2,1)S(1)} all-to-all(bf16[16,112,128]{2,1,0:T(8,128)(2,1)S(1)} %cross.1), channel_id=1, replica_groups=mesh['grp'=2,'sp'=16] {'sp'}, dimensions={0} | all-to-all | bytes 917504 | tf_op jit(solution)/shard_map/all_to_all | solution.py:305
  147.9 3.1 %finish.1 = bf16[1,6,64,1152]{3,2,1,0:T(8,128)(2,1)} custom-call(s32[1]{0:T(128)} %bitcast.device_ref, s32[1,6]{1,0:T(1,128)S(1)} %copy-done.8, s32[1,6]{1,0:T(1,128)S(1)} %copy-done.11, bf16[16,112,128]{2,1,0:T(8,128)(2,1)S(1)} %all_to_all.22.slots_ref, bf16[384,1152]{1,0:T(8,128)(2,1)S(1)} %get-tuple-element.8.middle_ref, bf16[576,1152]{1,0:T(8,128)(2,1)S(1)} %copy-done.5), custom_call_target="tpu_custom_call" | custom-call | tf_op jit(solution)/shard_map/finish/pallas_call | solution.py:293
  (10 shorter events, 0.0 us)
Async XLA Ops:
  0.0 2.1 %copy-start = (bf16[1152,1728]{0,1:T(8,128)(2,1)S(1)}, bf16[1152,1728]{0,1:T(8,128)(2,1)}, u32[]{:S(2)}) copy-start(bf16[1152,1728]{0,1:T(8,128)(2,1)} %param.13) | copy-start | bytes 11943940
  2.1 1.2 copy-start.2
  3.3 0.7 copy-start.7
  4.0 0.7 copy-start.9
  9.0 36.1 %copy-start.6 = (s32[1,6,8,8]{3,2,1,0:T(8,128)S(1)}, s32[1,6,8,8]{3,2,1,0:T(8,128)}, u32[]{:S(2)}) copy-start(s32[1,6,8,8]{3,2,1,0:T(8,128)} %mask_ref.1) | copy-start | bytes 4612
  9.0 36.1 %copy-start.8 = (s32[1,6]{1,0:T(1,128)S(1)}, s32[1,6]{1,0:T(1,128)}, u32[]{:S(2)}) copy-start(s32[1,6]{1,0:T(1,128)} %right_ref.9) | copy-start | bytes 76
  9.1 36.1 %copy-start.11 = (s32[1,6]{1,0:T(1,128)S(1)}, s32[1,6]{1,0:T(1,128)}, u32[]{:S(2)}) copy-start(s32[1,6]{1,0:T(1,128)} %lengths_ref.7) | copy-start | bytes 76
  9.1 36.1 %all-to-all-start = ((bf16[16,336,128]{2,1,0:T(8,128)(2,1)}), bf16[16,336,128]{2,1,0:T(8,128)(2,1)S(1)}, u32[]{:S(2)}, u32[]{:S(2)}) async-start(bf16[16,336,128]{2,1,0:T(8,128)(2,1)} %project.1), calls=%async_computation | async-start | bytes 2752512 | tf_op jit(solution)/shard_map/all_to_all | solution.py:305
  45.1 28.6 %copy-start.3 = (bf16[1,6,64,1152]{3,2,1,0:T(8,128)(2,1)S(1)}, bf16[1,6,64,1152]{3,2,1,0:T(8,128)(2,1)}, u32[]{:S(2)}) copy-start(bf16[1,6,64,1152]{3,2,1,0:T(8,128)(2,1)} %tokens_ref.3) | copy-start | bytes 2654212
  45.2 28.6 %copy-start.4 = (bf16[576,1152]{1,0:T(8,128)(2,1)S(1)}, bf16[576,1152]{1,0:T(8,128)(2,1)}, u32[]{:S(2)}) copy-start(bf16[576,1152]{1,0:T(8,128)(2,1)} %mix_ref.2) | copy-start | bytes 3981316
  45.2 28.6 %copy-start.10 = (f32[1152]{0:T(1024)S(1)}, f32[1152]{0:T(1024)}, u32[]{:S(2)}) copy-start(f32[1152]{0:T(1024)} %gain_ref.3) | copy-start | bytes 13828
  73.8 2.1 %copy-start.1 = (bf16[1152,1728]{0,1:T(8,128)(2,1)S(1)}, bf16[1152,1728]{0,1:T(8,128)(2,1)}, u32[]{:S(2)}) copy-start(bf16[1152,1728]{0,1:T(8,128)(2,1)} %param.16) | copy-start | bytes 11943940
  117.2 30.7 %copy-start.5 = (bf16[576,1152]{1,0:T(8,128)(2,1)S(1)}, bf16[576,1152]{1,0:T(8,128)(2,1)}, u32[]{:S(2)}) copy-start(bf16[576,1152]{1,0:T(8,128)(2,1)} %mix_ref.3) | copy-start | bytes 3981316

commit v2 on v1

--- a/solution.py
+++ b/solution.py
@@ -18,6 +18,7 @@
 QKV_ROWS = 336
 OUT_ROWS = 112
 NEG = -1e30
+FACTOR = HS**-0.5 * 1.4426950408889634
 VMEM = 24 * 1024 * 1024
 
 
@@ -52,37 +53,104 @@
     return (floats * lax.rsqrt(square + EPSILON) * gain[None, :]).astype(jnp.bfloat16)
 
 
-def project_and_pack(normed_ref, weight_ref, turned_ref, out_ref, cross):
-    inner = weight_ref.shape[0] // 3
-    turned_ref[...] = lax.dot_general(
-        weight_ref[...],
-        normed_ref[...],
-        (((1,), (1,)), ((), ())),
-        preferred_element_type=jnp.float32,
-    )
-    for head in range(HEADS):
-        for parity in range(2):
-            other = 1 - parity if cross else parity
+def project_and_pack(normed_ref, weights, slots_ref, copies_out, cross):
+    for pair, (copies, weight_ref) in enumerate(weights):
+        for copy in copies:
+            copy.wait()
+        turned = lax.dot_general(
+            weight_ref[...],
+            normed_ref[...],
+            (((1,), (1,)), ((), ())),
+            preferred_element_type=jnp.float32,
+        )
+        for inside in range(2):
 
             def item(which, m):
-                row = which * inner + head * HS
-                return turned_ref[row : row + HS, m * LANES : (m + 1) * LANES]
-
-            rows = [
-                side_by_side(item(0, m), parity, item(1, m), other) for m in range(3)
-            ]
-            rows.append(side_by_side(item(2, 0), other, item(2, 1), other))
-            rows.append(fold_third(item(2, 2), other))
-            rows.append(jnp.zeros((QKV_ROWS - 4 * HS - TOP, LANES), jnp.float32))
-            out_ref[head * 2 + parity] = jnp.concatenate(rows, axis=0).astype(jnp.bfloat16)
-
-
-def project_kernel(right_ref, tokens_ref, gain_ref, weight_ref, out_ref, normed_ref, turned_ref):
+                row = (which * 2 + inside) * HS
+                tile = turned[row : row + HS, m * LANES : (m + 1) * LANES]
+                return tile * FACTOR if which == 0 else tile
+
+            for parity in range(2):
+                other = 1 - parity if cross else parity
+                rows = [side_by_side(item(0, m), parity, item(1, m), other) for m in range(3)]
+                rows.append(side_by_side(item(2, 0), other, item(2, 1), other))
+                rows.append(fold_third(item(2, 2), other))
+                rows.append(jnp.zeros((QKV_ROWS - 4 * HS - TOP, LANES), jnp.float32))
+                slot = (pair * 2 + inside) * 2 + parity
+                slots_ref[slot] = jnp.concatenate(rows, axis=0).astype(jnp.bfloat16)
+        copies_out[pair].start()
+    for copy in copies_out:
+        copy.wait()
+
+
+def weight_copies(source_ref, held_ref, sems):
+    inner = source_ref.shape[0] // 3
+    pairs, rows, _ = held_ref.shape
+    rows = rows // 3
+    weights = []
+    for pair in range(pairs):
+        copies = [
+            pltpu.make_async_copy(
+                source_ref.at[pl.ds(which * inner + pair * rows, rows)],
+                held_ref.at[pair, pl.ds(which * rows, rows)],
+                sems.at[pair * 3 + which],
+            )
+            for which in range(3)
+        ]
+        weights.append((copies, held_ref.at[pair]))
+    return weights
+
+
+def slot_copies(slots_ref, out_ref, sems):
+    pairs = HEADS // 2
+    step = slots_ref.shape[0] // pairs
+    return [
+        pltpu.make_async_copy(
+            slots_ref.at[pl.ds(pair * step, step)],
+            out_ref.at[pl.ds(pair * step, step)],
+            sems.at[pair],
+        )
+        for pair in range(pairs)
+    ]
+
+
+def project_kernel(
+    right_hbm,
+    tokens_hbm,
+    gain_hbm,
+    weight_hbm,
+    out_hbm,
+    right_ref,
+    tokens_ref,
+    gain_ref,
+    weight_ref,
+    normed_ref,
+    slots_ref,
+    in_sems,
+    weight_sems,
+    out_sems,
+):
+    small = [
+        pltpu.make_async_copy(source, held, in_sems.at[i])
+        for i, (source, held) in enumerate(
+            [(right_hbm, right_ref), (gain_hbm, gain_ref), (tokens_hbm, tokens_ref)]
+        )
+    ]
+    weights = weight_copies(weight_hbm, weight_ref, weight_sems)
+    for copy in small:
+        copy.start()
+    for copies, _ in weights:
+        for copy in copies:
+            copy.start()
+    for copy in small:
+        copy.wait()
     order = cycle_order(right_ref)
     for j in range(6):
         floats = tokens_ref[0, order[j]].astype(jnp.float32)
         normed_ref[j * TILE : (j + 1) * TILE, :] = normalise(floats, gain_ref[...])
-    project_and_pack(normed_ref, weight_ref, turned_ref, out_ref, False)
+    project_and_pack(
+        normed_ref, weights, slots_ref, slot_copies(slots_ref, out_hbm, out_sems), False
+    )
 
 
 def unpack(slots_ref, key_bias, query_rows, query_ref, key_ref, value_ref):
@@ -118,18 +186,34 @@
             )
 
 
-def attend(query, parts):
-    factor = HS**-0.5 * 1.4426950408889634
-    scores = [jnp.dot(keys, query, preferred_element_type=jnp.float32) for keys, _ in parts]
-    top = functools.reduce(
-        jnp.maximum, [jnp.max(score, axis=0, keepdims=True) for score in scores]
-    )
-    total = None
-    for score, (_, values) in zip(scores, parts):
-        weights = jnp.exp2((score - top) * factor).astype(jnp.bfloat16)
-        term = jnp.dot(values, weights, preferred_element_type=jnp.float32)
-        total = term if total is None else total + term
-    return total[:HS] / total[HS : HS + 1]
+def attend(jobs, query_ref, key_ref, value_ref, attended_ref):
+    def scores(job):
+        m, lanes, parts = job
+        query = query_ref[m, :, lanes]
+        return [
+            jnp.dot(key_ref[n, span, :], query, preferred_element_type=jnp.float32)
+            for n, span in parts
+        ]
+
+    def finish(job, found):
+        m, lanes, parts = job
+        top = functools.reduce(
+            jnp.maximum, [jnp.max(score, axis=0, keepdims=True) for score in found]
+        )
+        total = None
+        for score, (n, span) in zip(found, parts):
+            weights = jnp.exp2(score - top).astype(jnp.bfloat16)
+            term = jnp.dot(value_ref[n, :, span], weights, preferred_element_type=jnp.float32)
+            total = term if total is None else total + term
+        attended_ref[m, :, lanes] = total[:HS] / total[HS : HS + 1]
+
+    ahead = None
+    for job in jobs:
+        found = scores(job)
+        if ahead is not None:
+            finish(*ahead)
+        ahead = (job, found)
+    finish(*ahead)
 
 
 def pack_outputs(attended_ref, out_ref):
@@ -175,6 +259,7 @@
 
     unpack(slots_ref, key_bias, query_rows, query_ref, key_ref, value_ref)
     wide = 2 * LANES
+    jobs = []
     for m in range(3):
         for i in range(blocks // 2):
             first = max(0, 2 * i - 2) * LANES
@@ -182,11 +267,8 @@
             spans = [slice(first, last)]
             if first > 0:
                 spans.append(slice(0, LANES))
-            lanes = slice(i * wide, (i + 1) * wide)
-            attended_ref[m, :, lanes] = attend(
-                query_ref[m, :, lanes],
-                [(key_ref[m, span, :], value_ref[m, :, span]) for span in spans],
-            )
+            jobs.append((m, slice(i * wide, (i + 1) * wide), [(m, span) for span in spans]))
+    attend(jobs, query_ref, key_ref, value_ref, attended_ref)
     pack_outputs(attended_ref, out_ref)
 
 
@@ -213,14 +295,13 @@
 
     unpack(slots_ref, key_bias, query_rows, query_ref, key_ref, value_ref)
     wide = 2 * LANES
+    every = slice(0, key_ref.shape[1])
+    jobs = []
     for m in range(3):
         second = jnp.where(parity == 0, (m + 2) % 3, (m + 1) % 3)
         for i in range(query_ref.shape[2] // wide):
-            lanes = slice(i * wide, (i + 1) * wide)
-            attended_ref[m, :, lanes] = attend(
-                query_ref[m, :, lanes],
-                [(key_ref[m], value_ref[m]), (key_ref[second], value_ref[second])],
-            )
+            jobs.append((m, slice(i * wide, (i + 1) * wide), [(m, every), (second, every)]))
+    attend(jobs, query_ref, key_ref, value_ref, attended_ref)
     pack_outputs(attended_ref, out_ref)
 
 
@@ -254,51 +335,82 @@
     tokens_ref,
     mix_ref,
     gain_ref,
+    weight_hbm,
+    middle_ref,
+    out_hbm,
+    merged_ref,
     weight_ref,
+    normed_ref,
+    sent_ref,
+    weight_sems,
+    out_sems,
+):
+    weights = weight_copies(weight_hbm, weight_ref, weight_sems)
+    for copies, _ in weights:
+        for copy in copies:
+            copy.start()
+    order = cycle_order(right_ref)
+    merge_heads(slots_ref, merged_ref)
+    branch = jnp.dot(merged_ref[...], mix_ref[...], preferred_element_type=jnp.float32)
+    for j in range(6):
+        rows = slice(j * TILE, (j + 1) * TILE)
+        live = live_rows(device_ref, lengths_ref[0, order[j]])
+        middle = tokens_ref[0, order[j]].astype(jnp.float32) + live * branch[rows]
+        middle = middle.astype(jnp.bfloat16)
+        middle_ref[rows, :] = middle
+        normed_ref[rows, :] = normalise(middle.astype(jnp.float32), gain_ref[...])
+    project_and_pack(
+        normed_ref, weights, sent_ref, slot_copies(sent_ref, out_hbm, out_sems), True
+    )
+
+
+def finish_kernel(
+    device_ref,
+    right_ref,
+    lengths_ref,
+    slots_ref,
     middle_ref,
-    out_ref,
+    mix_ref,
+    out_hbm,
     merged_ref,
-    normed_ref,
-    turned_ref,
+    result_ref,
+    sems,
 ):
     order = cycle_order(right_ref)
     merge_heads(slots_ref, merged_ref)
+    branch = jnp.dot(merged_ref[...], mix_ref[...], preferred_element_type=jnp.float32)
+    copies = []
     for j in range(6):
         rows = slice(j * TILE, (j + 1) * TILE)
-        branch = jnp.dot(merged_ref[rows, :], mix_ref[...], preferred_element_type=jnp.float32)
         live = live_rows(device_ref, lengths_ref[0, order[j]])
-        middle = (tokens_ref[0, order[j]].astype(jnp.float32) + live * branch).astype(jnp.bfloat16)
-        middle_ref[rows, :] = middle
-        normed_ref[rows, :] = normalise(middle.astype(jnp.float32), gain_ref[...])
-    project_and_pack(normed_ref, weight_ref, turned_ref, out_ref, True)
-
-
-def finish_kernel(
-    device_ref, right_ref, lengths_ref, slots_ref, middle_ref, mix_ref, out_ref, merged_ref
-):
-    order = cycle_order(right_ref)
-    merge_heads(slots_ref, merged_ref)
-    for j in range(6):
-        rows = slice(j * TILE, (j + 1) * TILE)
-        branch = jnp.dot(merged_ref[rows, :], mix_ref[...], preferred_element_type=jnp.float32)
-        live = live_rows(device_ref, lengths_ref[0, order[j]])
-        out_ref[0, order[j]] = (middle_ref[rows, :].astype(jnp.float32) + live * branch).astype(
-            jnp.bfloat16
-        )
-
-
-def call(kernel, scalars, arrays, out_shape, scratch, name):
-    smem = pl.BlockSpec(memory_space=pltpu.SMEM)
-    vmem = pl.BlockSpec(memory_space=pltpu.VMEM)
+        result = middle_ref[rows, :].astype(jnp.float32) + live * branch[rows]
+        result_ref[j] = result.astype(jnp.bfloat16)
+        copy = pltpu.make_async_copy(result_ref.at[j], out_hbm.at[0, order[j]], sems.at[j])
+        copy.start()
+        copies.append(copy)
+    for copy in copies:
+        copy.wait()
+
+
+SMEM_SPEC = pl.BlockSpec(memory_space=pltpu.SMEM)
+VMEM_SPEC = pl.BlockSpec(memory_space=pltpu.VMEM)
+HBM_SPEC = pl.BlockSpec(memory_space=pltpu.HBM)
+
+
+def in_hbm(array):
+    return pltpu.with_memory_space_constraint(array, pltpu.HBM)
+
+
+def call(kernel, in_specs, args, out_specs, out_shape, scratch, name):
     return pl.pallas_call(
         kernel,
         out_shape=out_shape,
-        in_specs=[smem] * len(scalars) + [vmem] * len(arrays),
-        out_specs=jax.tree.map(lambda _: vmem, out_shape),
+        in_specs=in_specs,
+        out_specs=out_specs,
         scratch_shapes=scratch,
         compiler_params=pltpu.CompilerParams(vmem_limit_bytes=VMEM),
         name=name,
-    )(*scalars, *arrays)
+    )(*args)
 
 
 def exchange(slots):
@@ -326,9 +438,13 @@
     device = lax.axis_index("sp").astype(jnp.int32).reshape(1)
     qkv_slots = jax.ShapeDtypeStruct((devices_sp, QKV_ROWS, LANES), jnp.bfloat16)
     out_slots = jax.ShapeDtypeStruct((devices_sp, OUT_ROWS, LANES), jnp.bfloat16)
-    turned = pltpu.VMEM((3 * inner, rows), jnp.float32)
     normed = pltpu.VMEM((rows, width), jnp.bfloat16)
     merged = pltpu.VMEM((rows, inner), jnp.bfloat16)
+    pairs = HEADS // 2
+    weights = pltpu.VMEM((pairs, 3 * inner // pairs, width), jnp.bfloat16)
+    slots_held = pltpu.VMEM(qkv_slots.shape, jnp.bfloat16)
+    weight_sems = pltpu.SemaphoreType.DMA((3 * pairs,))
+    slot_sems = pltpu.SemaphoreType.DMA((pairs,))
     heads = [
         pltpu.VMEM((3, LANES, view_len), jnp.bfloat16),
         pltpu.VMEM((3, view_len, LANES), jnp.bfloat16),
@@ -337,42 +453,66 @@
     ]
     slots = call(
         project_kernel,
-        [right_view],
-        [tokens, gain_spatial, qkv_spatial.T],
+        [HBM_SPEC] * 4,
+        [in_hbm(x) for x in (right_view, tokens, gain_spatial, qkv_spatial.T)],
+        HBM_SPEC,
         qkv_slots,
-        [normed, turned],
+        [
+            pltpu.SMEM(right_view.shape, jnp.int32),
+            pltpu.VMEM(tokens.shape, jnp.bfloat16),
+            pltpu.VMEM((width,), jnp.float32),
+            weights,
+            normed,
+            slots_held,
+            pltpu.SemaphoreType.DMA((3,)),
+            weight_sems,
+            slot_sems,
+        ],
         "project",
     )
     attended = call(
         spatial_kernel,
-        [device, right_view, lengths, window_mask],
-        [exchange(slots)],
+        [SMEM_SPEC] * 4 + [VMEM_SPEC],
+        [device, right_view, lengths, window_mask, exchange(slots)],
+        VMEM_SPEC,
         out_slots,
         heads,
         "spatial",
     )
     middle, slots = call(
         middle_kernel,
-        [device, right_view, lengths],
-        [exchange(attended), tokens, out_spatial, gain_cross, qkv_cross.T],
+        [SMEM_SPEC] * 3 + [VMEM_SPEC] * 4 + [HBM_SPEC],
+        [
+            device,
+            right_view,
+            lengths,
+            exchange(attended),
+            tokens,
+            out_spatial,
+            gain_cross,
+            in_hbm(qkv_cross.T),
+        ],
+        (VMEM_SPEC, HBM_SPEC),
         (jax.ShapeDtypeStruct((rows, width), jnp.bfloat16), qkv_slots),
-        [merged, normed, turned],
+        [merged, weights, normed, slots_held, weight_sems, slot_sems],
         "middle",
     )
     attended = call(
         cross_kernel,
-        [device, right_view, lengths],
-        [exchange(slots)],
+        [SMEM_SPEC] * 3 + [VMEM_SPEC],
+        [device, right_view, lengths, exchange(slots)],
+        VMEM_SPEC,
         out_slots,
         heads,
         "cross",
     )
     return call(
         finish_kernel,
-        [device, right_view, lengths],
-        [exchange(attended), middle, out_cross],
+        [SMEM_SPEC] * 3 + [VMEM_SPEC] * 3,
+        [device, right_view, lengths, exchange(attended), middle, out_cross],
+        HBM_SPEC,
         jax.ShapeDtypeStruct(tokens.shape, jnp.bfloat16),
-        [merged],
+        [merged, pltpu.VMEM((6, TILE, width), jnp.bfloat16), pltpu.SemaphoreType.DMA((6,))],
         "finish",
     )
 

time: 152 us -> 141 us (0.928)
  local copies, waits for them, and re-layouts: 6.8 us -> 0.04 us
  Pallas kernels: 33 us -> 29.5 us
    unnamed x24 -> x14, local copies, waits for them, and re-layouts: 6.8 us -> 0.04 us
    pallas_call x5, Pallas kernels: 33 us -> 29.5 us  [call(): pl.pallas_call(kernel, out_shape=out_shape, in_specs=in_specs, out_specs=...]
where the time goes in v2:
time: 141 us
  blocking collectives  75 us (53%)
  Pallas kernels  29.5 us (21%)
  waiting for transfers between devices  28.6 us (20%)
  starting transfers between devices  7.52 us (5%)
    all_to_all x3, blocking collectives, exchange(): return lax.all_to_all(slots, 'sp', split_axis=0, concat_axis=0, tiled=True)  75 us
    pallas_call x5, Pallas kernels, call(): pl.pallas_call(kernel, out_shape=out_shape, in_specs=in_specs, out_specs=...  29.5 us
    all_to_all x1, waiting for transfers between devices, exchange(): return lax.all_to_all(slots, 'sp', split_axis=0, concat_axis=0, tiled=True)  28.6 us
    all_to_all x1, starting transfers between devices, exchange(): return lax.all_to_all(slots, 'sp', split_axis=0, concat_axis=0, tiled=True)  7.52 us
  transfers between devices with their start and end apart: 1, of which 1 were waited for; matrix products, arithmetic and copies ran while one was open for 0% of the time, Pallas kernels for 0%

profile of v2, /device:TPU:0, one launch (start us, length us, event | category | flops | bytes accessed | tf_op | source)
XLA Modules:
  0.0 140.9 jit_solution(9525535480042887314)
XLA Ops:
  0.0 6.9 %project.1 = bf16[16,336,128]{2,1,0:T(8,128)(2,1)} custom-call(s32[1,6]{1,0:T(1,128)} %right_ref.7, bf16[1,6,64,1152]{3,2,1,0:T(8,128)(2,1)} %tokens_ref.1, f32[1152]{0:T(1024)} %gain_hbm.1, bf16[1728,1152]{1,0:T(8,128)(2,1)} %bitcast.3), custom_call_target="tpu_custom_call" | custom-call | tf_op jit(solution)/shard_map/project/pallas_call | solution.py:405
  6.9 0.0 copy-start.3
  6.9 0.0 copy-start.4
  6.9 0.0 copy-start.6
  6.9 7.5 %all-to-all-start = ((bf16[16,336,128]{2,1,0:T(8,128)(2,1)}), bf16[16,336,128]{2,1,0:T(8,128)(2,1)S(1)}, u32[]{:S(2)}, u32[]{:S(2)}) async-start(bf16[16,336,128]{2,1,0:T(8,128)(2,1)} %project.1), calls=%async_computation | async-start | bytes 2752512 | tf_op jit(solution)/shard_map/all_to_all | solution.py:417
  14.5 28.6 %all-to-all-done.slots_ref = bf16[16,336,128]{2,1,0:T(8,128)(2,1)S(1)} async-done(((bf16[16,336,128]{2,1,0:T(8,128)(2,1)}), bf16[16,336,128]{2,1,0:T(8,128)(2,1)S(1)}, u32[]{:S(2)}, u32[]{:S(2)}) %all-to-all-start) | async-done | bytes 1376288 | tf_op jit(solution)/shard_map/all_to_all | solution.py:417
  43.0 0.0 copy-done.3
  43.0 0.0 copy-done.4
  43.0 0.0 copy-done.6
  43.0 0.0 copy-start
  43.0 0.0 copy-start.1
  43.0 0.0 copy-start.5
  43.1 4.7 %spatial.1 = bf16[16,112,128]{2,1,0:T(8,128)(2,1)S(1)} custom-call(s32[1]{0:T(128)} %bitcast.device_ref, s32[1,6]{1,0:T(1,128)S(1)} %copy-done.4, s32[1,6]{1,0:T(1,128)S(1)} %copy-done.6, s32[1,6,8,8]{3,2,1,0:T(8,128)S(1)} %copy-done.3, bf16[16,336,128]{2,1,0:T(8,128)(2,1)S(1)} %all-to-all-done.slots_ref), custom_call_target="tpu_custom_call" | custom-call | tf_op jit(solution)/shard_map/spatial/pallas_call | solution.py:405
  47.8 21.3 %all_to_all.20.slots_ref = bf16[16,112,128]{2,1,0:T(8,128)(2,1)S(1)} all-to-all(bf16[16,112,128]{2,1,0:T(8,128)(2,1)S(1)} %spatial.1), channel_id=1, replica_groups=mesh['grp'=2,'sp'=16] {'sp'}, dimensions={0} | all-to-all | bytes 917504 | tf_op jit(solution)/shard_map/all_to_all | solution.py:417
  69.1 0.0 copy-done
  69.1 0.0 copy-done.1
  69.1 0.0 copy-done.5
  69.1 6.8 %middle.1 = (bf16[384,1152]{1,0:T(8,128)(2,1)S(1)}, bf16[16,336,128]{2,1,0:T(8,128)(2,1)S(1)}) custom-call(s32[1]{0:T(128)} %bitcast.device_ref, s32[1,6]{1,0:T(1,128)S(1)} %copy-done.4, s32[1,6]{1,0:T(1,128)S(1)} %copy-done.6, bf16[16,112,128]{2,1,0:T(8,128)(2,1)S(1)} %all_to_all.20.slots_ref, bf16[1,6,64,1152]{3,2,1,0:T(8,128)(2,1)S(1)} %copy-done, ...), custom_call_target="tpu_custom_call" | custom-call | tf_op jit(solution)/shard_map/middle/pallas_call | solution.py:405
  75.9 36.4 %all_to_all.21.slots_ref = bf16[16,336,128]{2,1,0:T(8,128)(2,1)S(1)} all-to-all(bf16[16,336,128]{2,1,0:T(8,128)(2,1)S(1)} %get-tuple-element.7), channel_id=1, replica_groups=mesh['grp'=2,'sp'=16] {'sp'}, dimensions={0} | all-to-all | bytes 2752512 | tf_op jit(solution)/shard_map/all_to_all | solution.py:417
  112.3 0.0 copy-start.2
  112.3 8.5 %cross.1 = bf16[16,112,128]{2,1,0:T(8,128)(2,1)S(1)} custom-call(s32[1]{0:T(128)} %bitcast.device_ref, s32[1,6]{1,0:T(1,128)S(1)} %copy-done.4, s32[1,6]{1,0:T(1,128)S(1)} %copy-done.6, bf16[16,336,128]{2,1,0:T(8,128)(2,1)S(1)} %all_to_all.21.slots_ref), custom_call_target="tpu_custom_call" | custom-call | tf_op jit(solution)/shard_map/cross/pallas_call | solution.py:405
  120.8 17.3 %all_to_all.22.slots_ref = bf16[16,112,128]{2,1,0:T(8,128)(2,1)S(1)} all-to-all(bf16[16,112,128]{2,1,0:T(8,128)(2,1)S(1)} %cross.1), channel_id=1, replica_groups=mesh['grp'=2,'sp'=16] {'sp'}, dimensions={0} | all-to-all | bytes 917504 | tf_op jit(solution)/shard_map/all_to_all | solution.py:417
  138.1 0.0 copy-done.2
  138.1 2.6 %finish.1 = bf16[1,6,64,1152]{3,2,1,0:T(8,128)(2,1)} custom-call(s32[1]{0:T(128)} %bitcast.device_ref, s32[1,6]{1,0:T(1,128)S(1)} %copy-done.4, s32[1,6]{1,0:T(1,128)S(1)} %copy-done.6, bf16[16,112,128]{2,1,0:T(8,128)(2,1)S(1)} %all_to_all.22.slots_ref, bf16[384,1152]{1,0:T(8,128)(2,1)S(1)} %get-tuple-element.8.middle_ref, bf16[576,1152]{1,0:T(8,128)(2,1)S(1)} %copy-done.2), custom_call_target="tpu_custom_call" | custom-call | tf_op jit(solution)/shard_map/finish/pallas_call | solution.py:405
Async XLA Ops:
  6.9 36.1 %copy-start.3 = (s32[1,6,8,8]{3,2,1,0:T(8,128)S(1)}, s32[1,6,8,8]{3,2,1,0:T(8,128)}, u32[]{:S(2)}) copy-start(s32[1,6,8,8]{3,2,1,0:T(8,128)} %mask_ref.1) | copy-start | bytes 4612
  6.9 36.1 %copy-start.4 = (s32[1,6]{1,0:T(1,128)S(1)}, s32[1,6]{1,0:T(1,128)}, u32[]{:S(2)}) copy-start(s32[1,6]{1,0:T(1,128)} %right_ref.7) | copy-start | bytes 76
  6.9 36.1 %copy-start.6 = (s32[1,6]{1,0:T(1,128)S(1)}, s32[1,6]{1,0:T(1,128)}, u32[]{:S(2)}) copy-start(s32[1,6]{1,0:T(1,128)} %lengths_ref.7) | copy-start | bytes 76
  6.9 36.1 %all-to-all-start = ((bf16[16,336,128]{2,1,0:T(8,128)(2,1)}), bf16[16,336,128]{2,1,0:T(8,128)(2,1)S(1)}, u32[]{:S(2)}, u32[]{:S(2)}) async-start(bf16[16,336,128]{2,1,0:T(8,128)(2,1)} %project.1), calls=%async_computation | async-start | bytes 2752512 | tf_op jit(solution)/shard_map/all_to_all | solution.py:417
  43.0 26.1 %copy-start = (bf16[1,6,64,1152]{3,2,1,0:T(8,128)(2,1)S(1)}, bf16[1,6,64,1152]{3,2,1,0:T(8,128)(2,1)}, u32[]{:S(2)}) copy-start(bf16[1,6,64,1152]{3,2,1,0:T(8,128)(2,1)} %tokens_ref.1) | copy-start | bytes 2654212
  43.0 26.1 %copy-start.1 = (bf16[576,1152]{1,0:T(8,128)(2,1)S(1)}, bf16[576,1152]{1,0:T(8,128)(2,1)}, u32[]{:S(2)}) copy-start(bf16[576,1152]{1,0:T(8,128)(2,1)} %mix_ref.2) | copy-start | bytes 3981316
  43.0 26.1 %copy-start.5 = (f32[1152]{0:T(1024)S(1)}, f32[1152]{0:T(1024)}, u32[]{:S(2)}) copy-start(f32[1152]{0:T(1024)} %gain_ref.1) | copy-start | bytes 13828
  112.3 25.8 %copy-start.2 = (bf16[576,1152]{1,0:T(8,128)(2,1)S(1)}, bf16[576,1152]{1,0:T(8,128)(2,1)}, u32[]{:S(2)}) copy-start(bf16[576,1152]{1,0:T(8,128)(2,1)} %mix_ref.3) | copy-start | bytes 3981316

commit v3 on v2

--- a/solution.py
+++ b/solution.py
@@ -15,10 +15,13 @@
 TILE = 64
 LANES = 128
 TOP = 40
-QKV_ROWS = 336
+QKV_ROWS = 328
 OUT_ROWS = 112
 NEG = -1e30
 FACTOR = HS**-0.5 * 1.4426950408889634
+FIRST_GROUPS = (4, 4)
+SECOND_GROUPS = (6, 2)
+AHEAD = 2
 VMEM = 24 * 1024 * 1024
 
 
@@ -53,65 +56,83 @@
     return (floats * lax.rsqrt(square + EPSILON) * gain[None, :]).astype(jnp.bfloat16)
 
 
-def project_and_pack(normed_ref, weights, slots_ref, copies_out, cross):
-    for pair, (copies, weight_ref) in enumerate(weights):
-        for copy in copies:
-            copy.wait()
-        turned = lax.dot_general(
+def project_and_pack(normed_ref, groups, slots_ref, cross, arrived, done):
+    def project(weight_ref):
+        return lax.dot_general(
             weight_ref[...],
             normed_ref[...],
             (((1,), (1,)), ((), ())),
             preferred_element_type=jnp.float32,
         )
-        for inside in range(2):
+
+    def pack(head, heads, turned):
+        for inside in range(heads):
 
             def item(which, m):
-                row = (which * 2 + inside) * HS
+                row = (which * heads + inside) * HS
                 tile = turned[row : row + HS, m * LANES : (m + 1) * LANES]
                 return tile * FACTOR if which == 0 else tile
 
             for parity in range(2):
                 other = 1 - parity if cross else parity
-                rows = [side_by_side(item(0, m), parity, item(1, m), other) for m in range(3)]
-                rows.append(side_by_side(item(2, 0), other, item(2, 1), other))
-                rows.append(fold_third(item(2, 2), other))
-                rows.append(jnp.zeros((QKV_ROWS - 4 * HS - TOP, LANES), jnp.float32))
-                slot = (pair * 2 + inside) * 2 + parity
+                views = [2, 0, 1] if cross and parity == 0 else [0, 1, 2]
+                rows = [
+                    side_by_side(item(0, m), parity, item(1, views[m]), other) for m in range(3)
+                ]
+                rows.append(side_by_side(item(2, views[0]), other, item(2, views[1]), other))
+                rows.append(fold_third(item(2, views[2]), other))
+                slot = (head + inside) * 2 + parity
                 slots_ref[slot] = jnp.concatenate(rows, axis=0).astype(jnp.bfloat16)
-        copies_out[pair].start()
-    for copy in copies_out:
+
+    ahead = None
+    for group, (head, heads, weight_ref) in enumerate(groups):
+        arrived(group)
+        turned = project(weight_ref)
+        if ahead is not None:
+            pack(*ahead)
+            done(group - 1)
+        ahead = (head, heads, turned)
+    pack(*ahead)
+    done(len(groups) - 1)
+
+
+def weight_groups(source_ref, held_ref, sems, sizes):
+    inner = source_ref.shape[0] // 3
+    copies, groups, head = [], [], 0
+    for group, heads in enumerate(sizes):
+        rows = heads * HS
+        copies.append(
+            [
+                pltpu.make_async_copy(
+                    source_ref.at[pl.ds(which * inner + head * HS, rows)],
+                    held_ref.at[pl.ds(3 * head * HS + which * rows, rows)],
+                    sems.at[group * 3 + which],
+                )
+                for which in range(3)
+            ]
+        )
+        groups.append((head, heads, held_ref.at[pl.ds(3 * head * HS, 3 * rows)]))
+        head += heads
+    return copies, groups
+
+
+def start_all(copies, priority=0):
+    for copy in copies:
+        copy.start(priority=priority)
+
+
+def wait_all(copies):
+    for copy in copies:
         copy.wait()
 
 
-def weight_copies(source_ref, held_ref, sems):
-    inner = source_ref.shape[0] // 3
-    pairs, rows, _ = held_ref.shape
-    rows = rows // 3
-    weights = []
-    for pair in range(pairs):
-        copies = [
-            pltpu.make_async_copy(
-                source_ref.at[pl.ds(which * inner + pair * rows, rows)],
-                held_ref.at[pair, pl.ds(which * rows, rows)],
-                sems.at[pair * 3 + which],
-            )
-            for which in range(3)
-        ]
-        weights.append((copies, held_ref.at[pair]))
-    return weights
-
-
-def slot_copies(slots_ref, out_ref, sems):
-    pairs = HEADS // 2
-    step = slots_ref.shape[0] // pairs
-    return [
-        pltpu.make_async_copy(
-            slots_ref.at[pl.ds(pair * step, step)],
-            out_ref.at[pl.ds(pair * step, step)],
-            sems.at[pair],
-        )
-        for pair in range(pairs)
-    ]
+def slot_copies(slots_ref, out_ref, sems, sizes):
+    copies, head = [], 0
+    for group, heads in enumerate(sizes):
+        span = pl.ds(2 * head, 2 * heads)
+        copies.append(pltpu.make_async_copy(slots_ref.at[span], out_ref.at[span], sems.at[group]))
+        head += heads
+    return copies
 
 
 def project_kernel(
@@ -131,33 +152,88 @@
     out_sems,
 ):
     small = [
-        pltpu.make_async_copy(source, held, in_sems.at[i])
-        for i, (source, held) in enumerate(
-            [(right_hbm, right_ref), (gain_hbm, gain_ref), (tokens_hbm, tokens_ref)]
+        pltpu.make_async_copy(right_hbm, right_ref, in_sems.at[0]),
+        pltpu.make_async_copy(gain_hbm, gain_ref, in_sems.at[1]),
+    ]
+    views = [
+        pltpu.make_async_copy(tokens_hbm.at[0, v], tokens_ref.at[0, v], in_sems.at[2 + v])
+        for v in range(6)
+    ]
+    copies, groups = weight_groups(weight_hbm, weight_ref, weight_sems, FIRST_GROUPS)
+    outgoing = slot_copies(slots_ref, out_hbm, out_sems, FIRST_GROUPS)
+    start_all(small)
+    start_all(views)
+    for group in range(min(AHEAD, len(groups))):
+        start_all(copies[group], 1)
+    wait_all(small)
+    order = cycle_order(right_ref)
+    place = [sum(jnp.where(order[j] == v, j, 0) for j in range(6)) for v in range(6)]
+    for v in range(6):
+        views[v].wait()
+        floats = tokens_ref[0, v].astype(jnp.float32)
+        rows = pl.ds(pl.multiple_of(place[v] * TILE, TILE), TILE)
+        normed_ref[rows, :] = normalise(floats, gain_ref[...])
+
+    def arrived(group):
+        wait_all(copies[group])
+        if group + AHEAD < len(groups):
+            start_all(copies[group + AHEAD], 1)
+
+    project_and_pack(
+        normed_ref, groups, slots_ref, False, arrived, lambda group: outgoing[group].start()
+    )
+    wait_all(outgoing)
+
+
+def prepare_kernel(
+    device_ref,
+    right_ref,
+    lengths_ref,
+    mask_ref,
+    tokens_ref,
+    _,
+    query_ref,
+    key_ref,
+    cross_ref,
+    live_ref,
+    ordered_ref,
+):
+    order = cycle_order(right_ref)
+    parity = device_ref[0] % 2
+    blocks = mask_ref.shape[-1]
+    view_len = key_ref.shape[-1]
+    position = lax.broadcasted_iota(jnp.int32, (8, view_len), 1)
+    first = lax.broadcasted_iota(jnp.int32, (8, view_len), 0) == 0
+    row8 = lax.broadcasted_iota(jnp.int32, (8, LANES), 0)
+
+    def keys_of(view):
+        return jnp.where(first & (position >= lengths_ref[0, view]), NEG, 0.0)
+
+    for m in range(3):
+        view = jnp.where(parity == 0, order[2 * m], order[2 * m + 1])
+        other = jnp.where(parity == 0, order[(2 * m - 1) % 6], order[2 * m])
+        key_ref[m] = keys_of(view)
+        cross_ref[m] = keys_of(other)
+        for b in range(blocks):
+            rows = jnp.zeros((8, LANES), jnp.float32)
+            for c in range(blocks):
+                addend = jnp.where(mask_ref[0, view, b, c] > 0, 0.0, NEG)
+                rows = jnp.where(row8 == c, addend, rows)
+            query_ref[m, :, b * LANES : (b + 1) * LANES] = rows
+    row = device_ref[0] * TILE + lax.broadcasted_iota(jnp.int32, (TILE, LANES), 0)
+    for j in range(6):
+        live_ref[j * TILE : (j + 1) * TILE, :] = jnp.where(
+            row < lengths_ref[0, order[j]], 1.0, 0.0
         )
-    ]
-    weights = weight_copies(weight_hbm, weight_ref, weight_sems)
-    for copy in small:
-        copy.start()
-    for copies, _ in weights:
-        for copy in copies:
-            copy.start()
-    for copy in small:
-        copy.wait()
-    order = cycle_order(right_ref)
-    for j in range(6):
-        floats = tokens_ref[0, order[j]].astype(jnp.float32)
-        normed_ref[j * TILE : (j + 1) * TILE, :] = normalise(floats, gain_ref[...])
-    project_and_pack(
-        normed_ref, weights, slots_ref, slot_copies(slots_ref, out_hbm, out_sems), False
-    )
-
-
-def unpack(slots_ref, key_bias, query_rows, query_ref, key_ref, value_ref):
+        ordered_ref[j * TILE : (j + 1) * TILE, :] = tokens_ref[0, order[j]]
+
+
+def unpack(slots_ref, bias_ref, rows_ref, query_ref, key_ref, value_ref):
     blocks = slots_ref.shape[0] // 2
     low = low_lanes(QKV_ROWS)
     row8 = lax.broadcasted_iota(jnp.int32, (8, LANES), 0)
     pad = jnp.zeros((LANES - HS - 16, LANES), jnp.float32)
+    zero = jnp.zeros((8, LANES), jnp.float32)
     first_row = jnp.where(row8 == 0, 1.0, 0.0)
     for b in range(blocks):
         span = slice(b * LANES, (b + 1) * LANES)
@@ -165,7 +241,7 @@
         odd = slots_ref[2 * b + 1].astype(jnp.float32)
         lower = jnp.where(low, even, swap(odd))
         upper = jnp.where(low, swap(even), odd)
-        own_block = jnp.where(row8 == b, 1.0, 0.0)
+        own_block = zero if rows_ref is None else jnp.where(row8 == b, 1.0, 0.0)
         values = [
             lower[3 * HS : 4 * HS],
             upper[3 * HS : 4 * HS],
@@ -174,12 +250,12 @@
             ),
         ]
         for m in range(3):
-            query = jnp.concatenate(
-                [lower[m * HS : (m + 1) * HS], query_rows(m, b, row8), first_row, pad], axis=0
+            rows = zero if rows_ref is None else rows_ref[m, :, span]
+            query = jnp.concatenate([lower[m * HS : (m + 1) * HS], rows, first_row, pad], axis=0)
+            query_ref[m, :, span] = query.astype(jnp.bfloat16)
+            key = jnp.concatenate(
+                [upper[m * HS : (m + 1) * HS], own_block, bias_ref[m, :, span], pad], axis=0
             )
-            query_ref[m, :, span] = query.astype(jnp.bfloat16)
-            live = jnp.where(row8 == 0, key_bias(m, b), 0.0)
-            key = jnp.concatenate([upper[m * HS : (m + 1) * HS], own_block, live, pad], axis=0)
             key_ref[m, span, :] = key.T.astype(jnp.bfloat16)
             value_ref[m, :, span] = jnp.concatenate([values[m], first_row], axis=0).astype(
                 jnp.bfloat16
@@ -225,39 +301,11 @@
             out_ref[2 * b + half] = jnp.concatenate(rows, axis=0).astype(jnp.bfloat16)
 
 
-def live_bias(length, b):
-    position = b * LANES + lax.broadcasted_iota(jnp.int32, (8, LANES), 1)
-    return jnp.where(position < length, 0.0, NEG)
-
-
 def spatial_kernel(
-    device_ref,
-    right_ref,
-    lengths_ref,
-    mask_ref,
-    slots_ref,
-    out_ref,
-    query_ref,
-    key_ref,
-    value_ref,
-    attended_ref,
+    slots_ref, rows_ref, bias_ref, out_ref, query_ref, key_ref, value_ref, attended_ref
 ):
-    order = cycle_order(right_ref)
-    parity = device_ref[0] % 2
-    views = [jnp.where(parity == 0, order[2 * m], order[2 * m + 1]) for m in range(3)]
-    blocks = mask_ref.shape[-1]
-
-    def query_rows(m, b, row8):
-        rows = jnp.zeros((8, LANES), jnp.float32)
-        for other in range(blocks):
-            allowed = mask_ref[0, views[m], b, other] > 0
-            rows = jnp.where(row8 == other, jnp.where(allowed, 0.0, NEG), rows)
-        return rows
-
-    def key_bias(m, b):
-        return live_bias(lengths_ref[0, views[m]], b)
-
-    unpack(slots_ref, key_bias, query_rows, query_ref, key_ref, value_ref)
+    unpack(slots_ref, bias_ref, rows_ref, query_ref, key_ref, value_ref)
+    blocks = slots_ref.shape[0] // 2
     wide = 2 * LANES
     jobs = []
     for m in range(3):
@@ -272,33 +320,13 @@
     pack_outputs(attended_ref, out_ref)
 
 
-def cross_kernel(
-    device_ref,
-    right_ref,
-    lengths_ref,
-    slots_ref,
-    out_ref,
-    query_ref,
-    key_ref,
-    value_ref,
-    attended_ref,
-):
-    order = cycle_order(right_ref)
-    parity = device_ref[0] % 2
-    views = [jnp.where(parity == 0, order[2 * m + 1], order[2 * m]) for m in range(3)]
-
-    def query_rows(m, b, row8):
-        return jnp.zeros((8, LANES), jnp.float32)
-
-    def key_bias(m, b):
-        return live_bias(lengths_ref[0, views[m]], b)
-
-    unpack(slots_ref, key_bias, query_rows, query_ref, key_ref, value_ref)
+def cross_kernel(slots_ref, bias_ref, out_ref, query_ref, key_ref, value_ref, attended_ref):
+    unpack(slots_ref, bias_ref, None, query_ref, key_ref, value_ref)
     wide = 2 * LANES
     every = slice(0, key_ref.shape[1])
     jobs = []
     for m in range(3):
-        second = jnp.where(parity == 0, (m + 2) % 3, (m + 1) % 3)
+        second = (m + 1) % 3
         for i in range(query_ref.shape[2] // wide):
             jobs.append((m, slice(i * wide, (i + 1) * wide), [(m, every), (second, every)]))
     attend(jobs, query_ref, key_ref, value_ref, attended_ref)
@@ -322,68 +350,59 @@
         merged_ref[m * LANES : (m + 1) * LANES, :] = merged.T.astype(jnp.bfloat16)
 
 
-def live_rows(device_ref, length):
-    position = device_ref[0] * TILE + lax.broadcasted_iota(jnp.int32, (TILE, 1), 0)
-    return (position < length).astype(jnp.float32)
-
-
 def middle_kernel(
-    device_ref,
-    right_ref,
-    lengths_ref,
     slots_ref,
     tokens_ref,
+    live_ref,
     mix_ref,
     gain_ref,
     weight_hbm,
     middle_ref,
-    out_hbm,
+    out_ref,
     merged_ref,
     weight_ref,
     normed_ref,
-    sent_ref,
     weight_sems,
-    out_sems,
 ):
-    weights = weight_copies(weight_hbm, weight_ref, weight_sems)
-    for copies, _ in weights:
-        for copy in copies:
-            copy.start()
-    order = cycle_order(right_ref)
+    copies, groups = weight_groups(weight_hbm, weight_ref, weight_sems, SECOND_GROUPS)
+    for group in copies:
+        start_all(group)
     merge_heads(slots_ref, merged_ref)
     branch = jnp.dot(merged_ref[...], mix_ref[...], preferred_element_type=jnp.float32)
     for j in range(6):
         rows = slice(j * TILE, (j + 1) * TILE)
-        live = live_rows(device_ref, lengths_ref[0, order[j]])
-        middle = tokens_ref[0, order[j]].astype(jnp.float32) + live * branch[rows]
+        middle = tokens_ref[rows, :].astype(jnp.float32) + live_ref[rows, :1] * branch[rows]
         middle = middle.astype(jnp.bfloat16)
         middle_ref[rows, :] = middle
         normed_ref[rows, :] = normalise(middle.astype(jnp.float32), gain_ref[...])
-    project_and_pack(
-        normed_ref, weights, sent_ref, slot_copies(sent_ref, out_hbm, out_sems), True
-    )
+    for group in copies:
+        wait_all(group)
+    project_and_pack(normed_ref, groups, out_ref, True, lambda group: None, lambda group: None)
 
 
 def finish_kernel(
-    device_ref,
-    right_ref,
-    lengths_ref,
+    right_hbm,
     slots_ref,
     middle_ref,
+    live_ref,
     mix_ref,
     out_hbm,
+    right_ref,
     merged_ref,
     result_ref,
+    right_sem,
     sems,
 ):
-    order = cycle_order(right_ref)
+    right_copy = pltpu.make_async_copy(right_hbm, right_ref, right_sem.at[0])
+    right_copy.start()
     merge_heads(slots_ref, merged_ref)
     branch = jnp.dot(merged_ref[...], mix_ref[...], preferred_element_type=jnp.float32)
+    right_copy.wait()
+    order = cycle_order(right_ref)
     copies = []
     for j in range(6):
         rows = slice(j * TILE, (j + 1) * TILE)
-        live = live_rows(device_ref, lengths_ref[0, order[j]])
-        result = middle_ref[rows, :].astype(jnp.float32) + live * branch[rows]
+        result = middle_ref[rows, :].astype(jnp.float32) + live_ref[rows, :1] * branch[rows]
         result_ref[j] = result.astype(jnp.bfloat16)
         copy = pltpu.make_async_copy(result_ref.at[j], out_hbm.at[0, order[j]], sems.at[j])
         copy.start()
@@ -440,11 +459,7 @@
     out_slots = jax.ShapeDtypeStruct((devices_sp, OUT_ROWS, LANES), jnp.bfloat16)
     normed = pltpu.VMEM((rows, width), jnp.bfloat16)
     merged = pltpu.VMEM((rows, inner), jnp.bfloat16)
-    pairs = HEADS // 2
-    weights = pltpu.VMEM((pairs, 3 * inner // pairs, width), jnp.bfloat16)
-    slots_held = pltpu.VMEM(qkv_slots.shape, jnp.bfloat16)
-    weight_sems = pltpu.SemaphoreType.DMA((3 * pairs,))
-    slot_sems = pltpu.SemaphoreType.DMA((pairs,))
+    weights = pltpu.VMEM((3 * inner, width), jnp.bfloat16)
     heads = [
         pltpu.VMEM((3, LANES, view_len), jnp.bfloat16),
         pltpu.VMEM((3, view_len, LANES), jnp.bfloat16),
@@ -463,17 +478,28 @@
             pltpu.VMEM((width,), jnp.float32),
             weights,
             normed,
-            slots_held,
-            pltpu.SemaphoreType.DMA((3,)),
-            weight_sems,
-            slot_sems,
+            pltpu.VMEM(qkv_slots.shape, jnp.bfloat16),
+            pltpu.SemaphoreType.DMA((8,)),
+            pltpu.SemaphoreType.DMA((3 * len(FIRST_GROUPS),)),
+            pltpu.SemaphoreType.DMA((len(FIRST_GROUPS),)),
         ],
         "project",
     )
+    per_view = jax.ShapeDtypeStruct((3, 8, view_len), jnp.float32)
+    stream = jax.ShapeDtypeStruct((rows, width), jnp.bfloat16)
+    block_rows, key_bias, cross_bias, live, ordered = call(
+        prepare_kernel,
+        [SMEM_SPEC] * 4 + [VMEM_SPEC, HBM_SPEC],
+        [device, right_view, lengths, window_mask, tokens, slots],
+        (VMEM_SPEC,) * 5,
+        (per_view, per_view, per_view, jax.ShapeDtypeStruct((rows, LANES), jnp.float32), stream),
+        [],
+        "prepare",
+    )
     attended = call(
         spatial_kernel,
-        [SMEM_SPEC] * 4 + [VMEM_SPEC],
-        [device, right_view, lengths, window_mask, exchange(slots)],
+        [VMEM_SPEC] * 3,
+        [exchange(slots), block_rows, key_bias],
         VMEM_SPEC,
         out_slots,
         heads,
@@ -481,26 +507,17 @@
     )
     middle, slots = call(
         middle_kernel,
-        [SMEM_SPEC] * 3 + [VMEM_SPEC] * 4 + [HBM_SPEC],
-        [
-            device,
-            right_view,
-            lengths,
-            exchange(attended),
-            tokens,
-            out_spatial,
-            gain_cross,
-            in_hbm(qkv_cross.T),
-        ],
-        (VMEM_SPEC, HBM_SPEC),
-        (jax.ShapeDtypeStruct((rows, width), jnp.bfloat16), qkv_slots),
-        [merged, weights, normed, slots_held, weight_sems, slot_sems],
+        [VMEM_SPEC] * 5 + [HBM_SPEC],
+        [exchange(attended), ordered, live, out_spatial, gain_cross, in_hbm(qkv_cross.T)],
+        (VMEM_SPEC, VMEM_SPEC),
+        (stream, qkv_slots),
+        [merged, weights, normed, pltpu.SemaphoreType.DMA((3 * len(SECOND_GROUPS),))],
         "middle",
     )
     attended = call(
         cross_kernel,
-        [SMEM_SPEC] * 3 + [VMEM_SPEC],
-        [device, right_view, lengths, exchange(slots)],
+        [VMEM_SPEC] * 2,
+        [exchange(slots), cross_bias],
         VMEM_SPEC,
         out_slots,
         heads,
@@ -508,11 +525,17 @@
     )
     return call(
         finish_kernel,
-        [SMEM_SPEC] * 3 + [VMEM_SPEC] * 3,
-        [device, right_view, lengths, exchange(attended), middle, out_cross],
+        [HBM_SPEC] + [VMEM_SPEC] * 4,
+        [in_hbm(right_view), exchange(attended), middle, live, out_cross],
         HBM_SPEC,
         jax.ShapeDtypeStruct(tokens.shape, jnp.bfloat16),
-        [merged, pltpu.VMEM((6, TILE, width), jnp.bfloat16), pltpu.SemaphoreType.DMA((6,))],
+        [
+            pltpu.SMEM(right_view.shape, jnp.int32),
+            merged,
+            pltpu.VMEM((6, TILE, width), jnp.bfloat16),
+            pltpu.SemaphoreType.DMA((1,)),
+            pltpu.SemaphoreType.DMA((6,)),
+        ],
         "finish",
     )
 

time: 141 us -> 136 us (0.965)
  waiting for transfers between devices: 28.6 us -> 26 us
  Pallas kernels: 29.5 us -> 27.1 us
    all_to_all x1, waiting for transfers between devices: 28.6 us -> 26 us  [exchange(): return lax.all_to_all(slots, 'sp', split_axis=0, concat_axis=0, tiled=True)]
    pallas_call x5 -> x6, Pallas kernels: 29.5 us -> 27.1 us  [call(): pl.pallas_call(kernel, out_shape=out_shape, in_specs=in_specs, out_specs=...]
  transfers between devices with their start and end apart: 1 -> 1, of which waited for: 1 -> 1; matrix products, arithmetic and copies ran while one was open for 0% -> 0% of each run, Pallas kernels for 0% -> 1%
where the time goes in v3:
time: 136 us
  blocking collectives  74.3 us (55%)
  Pallas kernels  27.1 us (20%)
  waiting for transfers between devices  26 us (19%)
  starting transfers between devices  7.52 us (6%)
    all_to_all x3, blocking collectives, exchange(): return lax.all_to_all(slots, 'sp', split_axis=0, concat_axis=0, tiled=True)  74.3 us
    pallas_call x6, Pallas kernels, call(): pl.pallas_call(kernel, out_shape=out_shape, in_specs=in_specs, out_specs=...  27.1 us
    all_to_all x1, waiting for transfers between devices, exchange(): return lax.all_to_all(slots, 'sp', split_axis=0, concat_axis=0, tiled=True)  26 us
    all_to_all x1, starting transfers between devices, exchange(): return lax.all_to_all(slots, 'sp', split_axis=0, concat_axis=0, tiled=True)  7.52 us
  transfers between devices with their start and end apart: 1, of which 1 were waited for; matrix products, arithmetic and copies ran while one was open for 0% of the time, Pallas kernels for 1%

profile of v3, /device:TPU:0, one launch (start us, length us, event | category | flops | bytes accessed | tf_op | source)
XLA Modules:
  0.0 135.9 jit_solution(10744302550703538590)
XLA Ops:
  0.0 5.7 %project.1._ = bf16[16,328,128]{2,1,0:T(8,128)(2,1)} custom-call(s32[1,6]{1,0:T(1,128)} %right_hbm.3, bf16[1,6,64,1152]{3,2,1,0:T(8,128)(2,1)} %tokens_ref.1, f32[1152]{0:T(1024)} %gain_hbm.1, bf16[1728,1152]{1,0:T(8,128)(2,1)} %bitcast.3), custom_call_target="tpu_custom_call" | custom-call | tf_op jit(solution)/shard_map/project/pallas_call | solution.py:424
  5.7 0.0 copy-start
  5.7 0.0 copy-start.5
  5.7 0.0 copy-start.7
  5.7 0.0 copy-start.8
  5.8 7.5 %all-to-all-start = ((bf16[16,328,128]{2,1,0:T(8,128)(2,1)}), bf16[16,328,128]{2,1,0:T(8,128)(2,1)S(1)}, u32[]{:S(2)}, u32[]{:S(2)}) async-start(bf16[16,328,128]{2,1,0:T(8,128)(2,1)} %project.1._), calls=%async_computation | async-start | bytes 2686976 | tf_op jit(solution)/shard_map/all_to_all | solution.py:436
  13.3 0.0 copy-done
  13.3 0.0 copy-done.5
  13.3 0.0 copy-done.7
  13.3 0.0 copy-done.8
  13.3 1.3 prepare.1
  14.6 0.0 copy-start.3
  14.6 0.6 copy-done.3
  15.2 26.0 %all-to-all-done.slots_ref = bf16[16,328,128]{2,1,0:T(8,128)(2,1)S(1)} async-done(((bf16[16,328,128]{2,1,0:T(8,128)(2,1)}), bf16[16,328,128]{2,1,0:T(8,128)(2,1)S(1)}, u32[]{:S(2)}, u32[]{:S(2)}) %all-to-all-start) | async-done | bytes 1343520 | tf_op jit(solution)/shard_map/all_to_all | solution.py:436
  41.3 3.7 %spatial.1 = bf16[16,112,128]{2,1,0:T(8,128)(2,1)S(1)} custom-call(bf16[16,328,128]{2,1,0:T(8,128)(2,1)S(1)} %all-to-all-done.slots_ref, f32[3,8,1024]{2,1,0:T(8,128)S(1)} %get-tuple-element.12.rows_ref, f32[3,8,1024]{2,1,0:T(8,128)S(1)} %get-tuple-element.13.bias_ref), custom_call_target="tpu_custom_call" | custom-call | tf_op jit(solution)/shard_map/spatial/pallas_call | solution.py:424
  45.0 21.2 %all_to_all.20.slots_ref = bf16[16,112,128]{2,1,0:T(8,128)(2,1)S(1)} all-to-all(bf16[16,112,128]{2,1,0:T(8,128)(2,1)S(1)} %spatial.1), channel_id=1, replica_groups=mesh['grp'=2,'sp'=16] {'sp'}, dimensions={0} | all-to-all | bytes 917504 | tf_op jit(solution)/shard_map/all_to_all | solution.py:436
  66.2 0.0 copy-done.6
  66.2 5.6 %middle.1 = (bf16[384,1152]{1,0:T(8,128)(2,1)S(1)}, bf16[16,328,128]{2,1,0:T(8,128)(2,1)S(1)}) custom-call(bf16[16,112,128]{2,1,0:T(8,128)(2,1)S(1)} %all_to_all.20.slots_ref, bf16[384,1152]{1,0:T(8,128)(2,1)S(1)} %get-tuple-element.14.tokens_ref, f32[384,128]{1,0:T(8,128)S(1)} %get-tuple-element.15.live_ref, bf16[576,1152]{1,0:T(8,128)(2,1)S(1)} %copy-done.1, ...), custom_call_target="tpu_custom_call" | custom-call | tf_op jit(solution)/shard_map/middle/pallas_call | solution.py:424
  71.8 0.0 copy-start.4
  71.8 35.9 %all_to_all.21.slots_ref = bf16[16,328,128]{2,1,0:T(8,128)(2,1)S(1)} all-to-all(bf16[16,328,128]{2,1,0:T(8,128)(2,1)S(1)} %get-tuple-element.16), channel_id=1, replica_groups=mesh['grp'=2,'sp'=16] {'sp'}, dimensions={0} | all-to-all | bytes 2686976 | tf_op jit(solution)/shard_map/all_to_all | solution.py:436
  107.7 0.0 copy-done.4
  107.7 8.3 %cross.1 = bf16[16,112,128]{2,1,0:T(8,128)(2,1)S(1)} custom-call(bf16[16,328,128]{2,1,0:T(8,128)(2,1)S(1)} %all_to_all.21.slots_ref, f32[3,8,1024]{2,1,0:T(8,128)S(1)} %copy-done.4), custom_call_target="tpu_custom_call" | custom-call | tf_op jit(solution)/shard_map/cross/pallas_call | solution.py:424
  116.0 17.2 %all_to_all.22.slots_ref = bf16[16,112,128]{2,1,0:T(8,128)(2,1)S(1)} all-to-all(bf16[16,112,128]{2,1,0:T(8,128)(2,1)S(1)} %cross.1), channel_id=1, replica_groups=mesh['grp'=2,'sp'=16] {'sp'}, dimensions={0} | all-to-all | bytes 917504 | tf_op jit(solution)/shard_map/all_to_all | solution.py:436
  133.2 2.6 %finish.1 = bf16[1,6,64,1152]{3,2,1,0:T(8,128)(2,1)} custom-call(s32[1,6]{1,0:T(1,128)} %right_hbm.3, bf16[16,112,128]{2,1,0:T(8,128)(2,1)S(1)} %all_to_all.22.slots_ref, bf16[384,1152]{1,0:T(8,128)(2,1)S(1)} %get-tuple-element.18.middle_ref, f32[384,128]{1,0:T(8,128)S(1)} %get-tuple-element.15.live_ref, bf16[576,1152]{1,0:T(8,128)(2,1)S(1)} %copy-done.2), custom_call_target="tpu_custom_call" | custom-call | tf_op jit(solution)/shard_map/finish/pallas_call | solution.py:424
  (5 shorter events, 0.0 us)
Async XLA Ops:
  5.7 7.6 %copy-start = (bf16[1,6,64,1152]{3,2,1,0:T(8,128)(2,1)S(1)}, bf16[1,6,64,1152]{3,2,1,0:T(8,128)(2,1)}, u32[]{:S(2)}) copy-start(bf16[1,6,64,1152]{3,2,1,0:T(8,128)(2,1)} %tokens_ref.1) | copy-start | bytes 2654212
  5.7 7.6 %copy-start.5 = (s32[1,6,8,8]{3,2,1,0:T(8,128)S(1)}, s32[1,6,8,8]{3,2,1,0:T(8,128)}, u32[]{:S(2)}) copy-start(s32[1,6,8,8]{3,2,1,0:T(8,128)} %mask_ref.1) | copy-start | bytes 4612
  5.7 7.6 %copy-start.7 = (s32[1,6]{1,0:T(1,128)S(1)}, s32[1,6]{1,0:T(1,128)}, u32[]{:S(2)}) copy-start(s32[1,6]{1,0:T(1,128)} %right_hbm.3) | copy-start | bytes 76
  5.7 7.6 %copy-start.8 = (s32[1,6]{1,0:T(1,128)S(1)}, s32[1,6]{1,0:T(1,128)}, u32[]{:S(2)}) copy-start(s32[1,6]{1,0:T(1,128)} %lengths_ref.1) | copy-start | bytes 76
  5.8 35.5 %all-to-all-start = ((bf16[16,328,128]{2,1,0:T(8,128)(2,1)}), bf16[16,328,128]{2,1,0:T(8,128)(2,1)S(1)}, u32[]{:S(2)}, u32[]{:S(2)}) async-start(bf16[16,328,128]{2,1,0:T(8,128)(2,1)} %project.1._), calls=%async_computation | async-start | bytes 2686976 | tf_op jit(solution)/shard_map/all_to_all | solution.py:436
  14.6 0.6 copy-start.3
  41.3 24.9 %copy-start.1 = (bf16[576,1152]{1,0:T(8,128)(2,1)S(1)}, bf16[576,1152]{1,0:T(8,128)(2,1)}, u32[]{:S(2)}) copy-start(bf16[576,1152]{1,0:T(8,128)(2,1)} %mix_ref.2) | copy-start | bytes 3981316
  41.3 24.9 %copy-start.6 = (f32[1152]{0:T(1024)S(1)}, f32[1152]{0:T(1024)}, u32[]{:S(2)}) copy-start(f32[1152]{0:T(1024)} %gain_ref.1) | copy-start | bytes 13828
  71.8 35.9 %copy-start.4 = (f32[3,8,1024]{2,1,0:T(8,128)S(1)}, f32[3,8,1024]{2,1,0:T(8,128)}, u32[]{:S(2)}) copy-start(f32[3,8,1024]{2,1,0:T(8,128)} %copy-done.3) | copy-start | bytes 294916
  107.7 25.4 %copy-start.2 = (bf16[576,1152]{1,0:T(8,128)(2,1)S(1)}, bf16[576,1152]{1,0:T(8,128)(2,1)}, u32[]{:S(2)}) copy-start(bf16[576,1152]{1,0:T(8,128)(2,1)} %mix_ref.3) | copy-start | bytes 3981316

commit v4 on v3

--- a/solution.py
+++ b/solution.py
@@ -19,8 +19,8 @@
 OUT_ROWS = 112
 NEG = -1e30
 FACTOR = HS**-0.5 * 1.4426950408889634
-FIRST_GROUPS = (4, 4)
-SECOND_GROUPS = (6, 2)
+FIRST_GROUPS = (2, 4, 2)
+SECOND_GROUPS = (8,)
 AHEAD = 2
 VMEM = 24 * 1024 * 1024
 
@@ -283,13 +283,13 @@
             total = term if total is None else total + term
         attended_ref[m, :, lanes] = total[:HS] / total[HS : HS + 1]
 
-    ahead = None
+    queue = []
     for job in jobs:
-        found = scores(job)
-        if ahead is not None:
-            finish(*ahead)
-        ahead = (job, found)
-    finish(*ahead)
+        queue.append((job, scores(job)))
+        if len(queue) > 2:
+            finish(*queue.pop(0))
+    for entry in queue:
+        finish(*entry)
 
 
 def pack_outputs(attended_ref, out_ref):

time: 136 us -> 135 us (level)
  no operation moved by 1% of the time
where the time goes in v4:
time: 135 us
  blocking collectives  74.3 us (55%)
  Pallas kernels  26 us (19%)
  waiting for transfers between devices  26 us (19%)
  starting transfers between devices  7.53 us (6%)
    all_to_all x3, blocking collectives, exchange(): return lax.all_to_all(slots, 'sp', split_axis=0, concat_axis=0, tiled=True)  74.3 us
    all_to_all x1, waiting for transfers between devices, exchange(): return lax.all_to_all(slots, 'sp', split_axis=0, concat_axis=0, tiled=True)  26 us
    pallas_call x6, Pallas kernels, call(): pl.pallas_call(kernel, out_shape=out_shape, in_specs=in_specs, out_specs=...  26 us
    all_to_all x1, starting transfers between devices, exchange(): return lax.all_to_all(slots, 'sp', split_axis=0, concat_axis=0, tiled=True)  7.53 us
  transfers between devices with their start and end apart: 1, of which 1 were waited for; matrix products, arithmetic and copies ran while one was open for 0% of the time, Pallas kernels for 1%

profile of v4, /device:TPU:0, one launch (start us, length us, event | category | flops | bytes accessed | tf_op | source)
XLA Modules:
  0.0 134.8 jit_solution(15048968729686235695)
XLA Ops:
  0.0 5.6 %project.1._ = bf16[16,328,128]{2,1,0:T(8,128)(2,1)} custom-call(s32[1,6]{1,0:T(1,128)} %right_hbm.3, bf16[1,6,64,1152]{3,2,1,0:T(8,128)(2,1)} %tokens_ref.1, f32[1152]{0:T(1024)} %gain_hbm.1, bf16[1728,1152]{1,0:T(8,128)(2,1)} %bitcast.3), custom_call_target="tpu_custom_call" | custom-call | tf_op jit(solution)/shard_map/project/pallas_call | solution.py:424
  5.6 0.0 copy-start
  5.6 0.0 copy-start.5
  5.7 0.0 copy-start.7
  5.7 0.0 copy-start.8
  5.7 7.5 %all-to-all-start = ((bf16[16,328,128]{2,1,0:T(8,128)(2,1)}), bf16[16,328,128]{2,1,0:T(8,128)(2,1)S(1)}, u32[]{:S(2)}, u32[]{:S(2)}) async-start(bf16[16,328,128]{2,1,0:T(8,128)(2,1)} %project.1._), calls=%async_computation | async-start | bytes 2686976 | tf_op jit(solution)/shard_map/all_to_all | solution.py:436
  13.2 0.0 copy-done
  13.2 0.0 copy-done.5
  13.2 0.0 copy-done.7
  13.3 0.0 copy-done.8
  13.3 1.3 prepare.1
  14.5 0.0 copy-start.3
  14.5 0.6 copy-done.3
  15.2 26.0 %all-to-all-done.slots_ref = bf16[16,328,128]{2,1,0:T(8,128)(2,1)S(1)} async-done(((bf16[16,328,128]{2,1,0:T(8,128)(2,1)}), bf16[16,328,128]{2,1,0:T(8,128)(2,1)S(1)}, u32[]{:S(2)}, u32[]{:S(2)}) %all-to-all-start) | async-done | bytes 1343520 | tf_op jit(solution)/shard_map/all_to_all | solution.py:436
  41.2 3.3 %spatial.1 = bf16[16,112,128]{2,1,0:T(8,128)(2,1)S(1)} custom-call(bf16[16,328,128]{2,1,0:T(8,128)(2,1)S(1)} %all-to-all-done.slots_ref, f32[3,8,1024]{2,1,0:T(8,128)S(1)} %get-tuple-element.12.rows_ref, f32[3,8,1024]{2,1,0:T(8,128)S(1)} %get-tuple-element.13.bias_ref), custom_call_target="tpu_custom_call" | custom-call | tf_op jit(solution)/shard_map/spatial/pallas_call | solution.py:424
  44.5 21.2 %all_to_all.20.slots_ref = bf16[16,112,128]{2,1,0:T(8,128)(2,1)S(1)} all-to-all(bf16[16,112,128]{2,1,0:T(8,128)(2,1)S(1)} %spatial.1), channel_id=1, replica_groups=mesh['grp'=2,'sp'=16] {'sp'}, dimensions={0} | all-to-all | bytes 917504 | tf_op jit(solution)/shard_map/all_to_all | solution.py:436
  65.7 0.0 copy-done.1
  65.7 0.0 copy-done.6
  65.7 5.6 %middle.1 = (bf16[384,1152]{1,0:T(8,128)(2,1)S(1)}, bf16[16,328,128]{2,1,0:T(8,128)(2,1)S(1)}) custom-call(bf16[16,112,128]{2,1,0:T(8,128)(2,1)S(1)} %all_to_all.20.slots_ref, bf16[384,1152]{1,0:T(8,128)(2,1)S(1)} %get-tuple-element.14.tokens_ref, f32[384,128]{1,0:T(8,128)S(1)} %get-tuple-element.15.live_ref, bf16[576,1152]{1,0:T(8,128)(2,1)S(1)} %copy-done.1, ...), custom_call_target="tpu_custom_call" | custom-call | tf_op jit(solution)/shard_map/middle/pallas_call | solution.py:424
  71.3 0.0 copy-start.4
  71.3 35.9 %all_to_all.21.slots_ref = bf16[16,328,128]{2,1,0:T(8,128)(2,1)S(1)} all-to-all(bf16[16,328,128]{2,1,0:T(8,128)(2,1)S(1)} %get-tuple-element.16), channel_id=1, replica_groups=mesh['grp'=2,'sp'=16] {'sp'}, dimensions={0} | all-to-all | bytes 2686976 | tf_op jit(solution)/shard_map/all_to_all | solution.py:436
  107.2 7.7 %cross.1 = bf16[16,112,128]{2,1,0:T(8,128)(2,1)S(1)} custom-call(bf16[16,328,128]{2,1,0:T(8,128)(2,1)S(1)} %all_to_all.21.slots_ref, f32[3,8,1024]{2,1,0:T(8,128)S(1)} %copy-done.4), custom_call_target="tpu_custom_call" | custom-call | tf_op jit(solution)/shard_map/cross/pallas_call | solution.py:424
  114.9 17.2 %all_to_all.22.slots_ref = bf16[16,112,128]{2,1,0:T(8,128)(2,1)S(1)} all-to-all(bf16[16,112,128]{2,1,0:T(8,128)(2,1)S(1)} %cross.1), channel_id=1, replica_groups=mesh['grp'=2,'sp'=16] {'sp'}, dimensions={0} | all-to-all | bytes 917504 | tf_op jit(solution)/shard_map/all_to_all | solution.py:436
  132.1 2.6 %finish.1 = bf16[1,6,64,1152]{3,2,1,0:T(8,128)(2,1)} custom-call(s32[1,6]{1,0:T(1,128)} %right_hbm.3, bf16[16,112,128]{2,1,0:T(8,128)(2,1)S(1)} %all_to_all.22.slots_ref, bf16[384,1152]{1,0:T(8,128)(2,1)S(1)} %get-tuple-element.18.middle_ref, f32[384,128]{1,0:T(8,128)S(1)} %get-tuple-element.15.live_ref, bf16[576,1152]{1,0:T(8,128)(2,1)S(1)} %copy-done.2), custom_call_target="tpu_custom_call" | custom-call | tf_op jit(solution)/shard_map/finish/pallas_call | solution.py:424
  (5 shorter events, 0.0 us)
Async XLA Ops:
  5.6 7.6 %copy-start = (bf16[1,6,64,1152]{3,2,1,0:T(8,128)(2,1)S(1)}, bf16[1,6,64,1152]{3,2,1,0:T(8,128)(2,1)}, u32[]{:S(2)}) copy-start(bf16[1,6,64,1152]{3,2,1,0:T(8,128)(2,1)} %tokens_ref.1) | copy-start | bytes 2654212
  5.6 7.6 %copy-start.5 = (s32[1,6,8,8]{3,2,1,0:T(8,128)S(1)}, s32[1,6,8,8]{3,2,1,0:T(8,128)}, u32[]{:S(2)}) copy-start(s32[1,6,8,8]{3,2,1,0:T(8,128)} %mask_ref.1) | copy-start | bytes 4612
  5.7 7.6 %copy-start.7 = (s32[1,6]{1,0:T(1,128)S(1)}, s32[1,6]{1,0:T(1,128)}, u32[]{:S(2)}) copy-start(s32[1,6]{1,0:T(1,128)} %right_hbm.3) | copy-start | bytes 76
  5.7 7.6 %copy-start.8 = (s32[1,6]{1,0:T(1,128)S(1)}, s32[1,6]{1,0:T(1,128)}, u32[]{:S(2)}) copy-start(s32[1,6]{1,0:T(1,128)} %lengths_ref.1) | copy-start | bytes 76
  5.7 35.5 %all-to-all-start = ((bf16[16,328,128]{2,1,0:T(8,128)(2,1)}), bf16[16,328,128]{2,1,0:T(8,128)(2,1)S(1)}, u32[]{:S(2)}, u32[]{:S(2)}) async-start(bf16[16,328,128]{2,1,0:T(8,128)(2,1)} %project.1._), calls=%async_computation | async-start | bytes 2686976 | tf_op jit(solution)/shard_map/all_to_all | solution.py:436
  14.5 0.6 copy-start.3
  41.2 24.5 %copy-start.1 = (bf16[576,1152]{1,0:T(8,128)(2,1)S(1)}, bf16[576,1152]{1,0:T(8,128)(2,1)}, u32[]{:S(2)}) copy-start(bf16[576,1152]{1,0:T(8,128)(2,1)} %mix_ref.2) | copy-start | bytes 3981316
  41.2 24.5 %copy-start.6 = (f32[1152]{0:T(1024)S(1)}, f32[1152]{0:T(1024)}, u32[]{:S(2)}) copy-start(f32[1152]{0:T(1024)} %gain_ref.1) | copy-start | bytes 13828
  71.3 35.9 %copy-start.4 = (f32[3,8,1024]{2,1,0:T(8,128)S(1)}, f32[3,8,1024]{2,1,0:T(8,128)}, u32[]{:S(2)}) copy-start(f32[3,8,1024]{2,1,0:T(8,128)} %copy-done.3) | copy-start | bytes 294916
  107.2 24.9 %copy-start.2 = (bf16[576,1152]{1,0:T(8,128)(2,1)S(1)}, bf16[576,1152]{1,0:T(8,128)(2,1)}, u32[]{:S(2)}) copy-start(bf16[576,1152]{1,0:T(8,128)(2,1)} %mix_ref.3) | copy-start | bytes 3981316

commit v5 on v4

--- a/solution.py
+++ b/solution.py
@@ -18,6 +18,8 @@
 QKV_ROWS = 328
 OUT_ROWS = 112
 NEG = -1e30
+ORDER = (9, 1, 5, 12, 0, 2, 7, 8, 14, 6, 4, 3, 15, 11, 10, 13)
+PLACE = tuple(ORDER.index(device) for device in range(len(ORDER)))
 FACTOR = HS**-0.5 * 1.4426950408889634
 FIRST_GROUPS = (2, 4, 2)
 SECOND_GROUPS = (8,)
@@ -81,7 +83,7 @@
                 ]
                 rows.append(side_by_side(item(2, views[0]), other, item(2, views[1]), other))
                 rows.append(fold_third(item(2, views[2]), other))
-                slot = (head + inside) * 2 + parity
+                slot = PLACE[(head + inside) * 2 + parity]
                 slots_ref[slot] = jnp.concatenate(rows, axis=0).astype(jnp.bfloat16)
 
     ahead = None
@@ -128,9 +130,14 @@
 
 def slot_copies(slots_ref, out_ref, sems, sizes):
     copies, head = [], 0
-    for group, heads in enumerate(sizes):
-        span = pl.ds(2 * head, 2 * heads)
-        copies.append(pltpu.make_async_copy(slots_ref.at[span], out_ref.at[span], sems.at[group]))
+    for heads in sizes:
+        places = PLACE[2 * head : 2 * (head + heads)]
+        copies.append(
+            [
+                pltpu.make_async_copy(slots_ref.at[place], out_ref.at[place], sems.at[place])
+                for place in places
+            ]
+        )
         head += heads
     return copies
 
@@ -180,9 +187,10 @@
             start_all(copies[group + AHEAD], 1)
 
     project_and_pack(
-        normed_ref, groups, slots_ref, False, arrived, lambda group: outgoing[group].start()
-    )
-    wait_all(outgoing)
+        normed_ref, groups, slots_ref, False, arrived, lambda group: start_all(outgoing[group])
+    )
+    for group in outgoing:
+        wait_all(group)
 
 
 def prepare_kernel(
@@ -237,8 +245,8 @@
     first_row = jnp.where(row8 == 0, 1.0, 0.0)
     for b in range(blocks):
         span = slice(b * LANES, (b + 1) * LANES)
-        even = slots_ref[2 * b].astype(jnp.float32)
-        odd = slots_ref[2 * b + 1].astype(jnp.float32)
+        even = slots_ref[PLACE[2 * b]].astype(jnp.float32)
+        odd = slots_ref[PLACE[2 * b + 1]].astype(jnp.float32)
         lower = jnp.where(low, even, swap(odd))
         upper = jnp.where(low, swap(even), odd)
         own_block = zero if rows_ref is None else jnp.where(row8 == b, 1.0, 0.0)
@@ -298,7 +306,7 @@
         tiles = [attended_ref[m, :, span] for m in range(3)]
         for half in range(2):
             rows = [side_by_side(tiles[0], half, tiles[1], half), fold_third(tiles[2], half)]
-            out_ref[2 * b + half] = jnp.concatenate(rows, axis=0).astype(jnp.bfloat16)
+            out_ref[PLACE[2 * b + half]] = jnp.concatenate(rows, axis=0).astype(jnp.bfloat16)
 
 
 def spatial_kernel(
@@ -337,8 +345,8 @@
     low = low_lanes(OUT_ROWS)
     tiles = [[], [], []]
     for head in range(HEADS):
-        even = slots_ref[2 * head].astype(jnp.float32)
-        odd = slots_ref[2 * head + 1].astype(jnp.float32)
+        even = slots_ref[PLACE[2 * head]].astype(jnp.float32)
+        odd = slots_ref[PLACE[2 * head + 1]].astype(jnp.float32)
         lower = jnp.where(low, even, swap(odd))
         upper = jnp.where(low, swap(even), odd)
         tiles[0].append(lower[:HS])
@@ -433,7 +441,9 @@
 
 
 def exchange(slots):
-    return lax.all_to_all(slots, "sp", split_axis=0, concat_axis=0, tiled=True)
+    return lax.all_to_all(
+        slots, "sp", split_axis=0, concat_axis=0, tiled=True, axis_index_groups=[list(ORDER)]
+    )
 
 
 def fast_shards(
@@ -481,7 +491,7 @@
             pltpu.VMEM(qkv_slots.shape, jnp.bfloat16),
             pltpu.SemaphoreType.DMA((8,)),
             pltpu.SemaphoreType.DMA((3 * len(FIRST_GROUPS),)),
-            pltpu.SemaphoreType.DMA((len(FIRST_GROUPS),)),
+            pltpu.SemaphoreType.DMA((devices_sp,)),
         ],
         "project",
     )

time: 135 us -> 131 us (0.970)
  blocking collectives: 74.3 us -> 69.4 us
    all_to_all x3, blocking collectives: 74.3 us -> 69.4 us  [exchange(): lax.all_to_all(slots, 'sp', split_axis=0, concat_axis=0, tiled=True, axis...]
where the time goes in v5:
time: 131 us; the launch traced here: 130 us
  blocking collectives  69.4 us (53%)
  Pallas kernels  26.2 us (20%)
  waiting for transfers between devices  25.9 us (20%)
  starting transfers between devices  7.76 us (6%)
    all_to_all x3, blocking collectives, exchange(): lax.all_to_all(slots, 'sp', split_axis=0, concat_axis=0, tiled=True, axis...  69.4 us
    pallas_call x6, Pallas kernels, call(): pl.pallas_call(kernel, out_shape=out_shape, in_specs=in_specs, out_specs=...  26.2 us
    all_to_all x1, waiting for transfers between devices, exchange(): lax.all_to_all(slots, 'sp', split_axis=0, concat_axis=0, tiled=True, axis...  25.9 us
    all_to_all x1, starting transfers between devices, exchange(): lax.all_to_all(slots, 'sp', split_axis=0, concat_axis=0, tiled=True, axis...  7.76 us
  transfers between devices with their start and end apart: 1, of which 1 were waited for; matrix products, arithmetic and copies ran while one was open for 0% of the time, Pallas kernels for 1%

profile of v5, /device:TPU:0, one launch (start us, length us, event | category | flops | bytes accessed | tf_op | source)
XLA Modules:
  0.0 130.2 jit_solution(13134517419748056644)
XLA Ops:
  0.0 5.8 %project.1._ = bf16[16,328,128]{2,1,0:T(8,128)(2,1)} custom-call(s32[1,6]{1,0:T(1,128)} %right_hbm.3, bf16[1,6,64,1152]{3,2,1,0:T(8,128)(2,1)} %tokens_ref.1, f32[1152]{0:T(1024)} %gain_hbm.1, bf16[1728,1152]{1,0:T(8,128)(2,1)} %bitcast.3), custom_call_target="tpu_custom_call" | custom-call | tf_op jit(solution)/shard_map/project/pallas_call | solution.py:432
  5.8 0.0 copy-start
  5.8 0.0 copy-start.5
  5.8 0.0 copy-start.7
  5.8 0.0 copy-start.8
  5.8 7.8 %all-to-all-start = ((bf16[16,328,128]{2,1,0:T(8,128)(2,1)}), bf16[16,328,128]{2,1,0:T(8,128)(2,1)S(1)}, u32[]{:S(2)}, u32[]{:S(2)}) async-start(bf16[16,328,128]{2,1,0:T(8,128)(2,1)} %project.1._), calls=%async_computation | async-start | bytes 2686976 | tf_op jit(solution)/shard_map/all_to_all | solution.py:444
  13.6 0.0 copy-done
  13.6 0.0 copy-done.5
  13.6 0.0 copy-done.7
  13.6 0.0 copy-done.8
  13.6 1.3 prepare.1
  14.9 0.0 copy-start.3
  14.9 0.6 copy-done.3
  15.5 25.9 %all-to-all-done.slots_ref = bf16[16,328,128]{2,1,0:T(8,128)(2,1)S(1)} async-done(((bf16[16,328,128]{2,1,0:T(8,128)(2,1)}), bf16[16,328,128]{2,1,0:T(8,128)(2,1)S(1)}, u32[]{:S(2)}, u32[]{:S(2)}) %all-to-all-start) | async-done | bytes 1343520 | tf_op jit(solution)/shard_map/all_to_all | solution.py:444
  41.4 3.2 %spatial.1 = bf16[16,112,128]{2,1,0:T(8,128)(2,1)S(1)} custom-call(bf16[16,328,128]{2,1,0:T(8,128)(2,1)S(1)} %all-to-all-done.slots_ref, f32[3,8,1024]{2,1,0:T(8,128)S(1)} %get-tuple-element.12.rows_ref, f32[3,8,1024]{2,1,0:T(8,128)S(1)} %get-tuple-element.13.bias_ref), custom_call_target="tpu_custom_call" | custom-call | tf_op jit(solution)/shard_map/spatial/pallas_call | solution.py:432
  44.7 18.0 %all_to_all.20.slots_ref = bf16[16,112,128]{2,1,0:T(8,128)(2,1)S(1)} all-to-all(bf16[16,112,128]{2,1,0:T(8,128)(2,1)S(1)} %spatial.1), channel_id=1, replica_groups={{9,1,5,12,0,2,7,8,14,6,4,3,15,11,10,13},{25,17,21,28,16,18,23,24,30,22,..., dimensions={0} | all-to-all | bytes 917504 | tf_op jit(solution)/shard_map/all_to_all | solution.py:444
  62.6 0.0 copy-done.1
  62.6 0.0 copy-done.6
  62.6 5.6 %middle.1 = (bf16[384,1152]{1,0:T(8,128)(2,1)S(1)}, bf16[16,328,128]{2,1,0:T(8,128)(2,1)S(1)}) custom-call(bf16[16,112,128]{2,1,0:T(8,128)(2,1)S(1)} %all_to_all.20.slots_ref, bf16[384,1152]{1,0:T(8,128)(2,1)S(1)} %get-tuple-element.14.tokens_ref, f32[384,128]{1,0:T(8,128)S(1)} %get-tuple-element.15.live_ref, bf16[576,1152]{1,0:T(8,128)(2,1)S(1)} %copy-done.1, ...), custom_call_target="tpu_custom_call" | custom-call | tf_op jit(solution)/shard_map/middle/pallas_call | solution.py:432
  68.2 0.0 copy-start.4
  68.2 35.7 %all_to_all.21.slots_ref = bf16[16,328,128]{2,1,0:T(8,128)(2,1)S(1)} all-to-all(bf16[16,328,128]{2,1,0:T(8,128)(2,1)S(1)} %get-tuple-element.16), channel_id=1, replica_groups={{9,1,5,12,0,2,7,8,14,6,4,3,15,11,10,13},{25,17,21,28,16,18,23,24,30,22,..., dimensions={0} | all-to-all | bytes 2686976 | tf_op jit(solution)/shard_map/all_to_all | solution.py:444
  104.0 7.7 %cross.1 = bf16[16,112,128]{2,1,0:T(8,128)(2,1)S(1)} custom-call(bf16[16,328,128]{2,1,0:T(8,128)(2,1)S(1)} %all_to_all.21.slots_ref, f32[3,8,1024]{2,1,0:T(8,128)S(1)} %copy-done.4), custom_call_target="tpu_custom_call" | custom-call | tf_op jit(solution)/shard_map/cross/pallas_call | solution.py:432
  111.7 15.7 %all_to_all.22.slots_ref = bf16[16,112,128]{2,1,0:T(8,128)(2,1)S(1)} all-to-all(bf16[16,112,128]{2,1,0:T(8,128)(2,1)S(1)} %cross.1), channel_id=1, replica_groups={{9,1,5,12,0,2,7,8,14,6,4,3,15,11,10,13},{25,17,21,28,16,18,23,24,30,22,..., dimensions={0} | all-to-all | bytes 917504 | tf_op jit(solution)/shard_map/all_to_all | solution.py:444
  127.5 2.6 %finish.1 = bf16[1,6,64,1152]{3,2,1,0:T(8,128)(2,1)} custom-call(s32[1,6]{1,0:T(1,128)} %right_hbm.3, bf16[16,112,128]{2,1,0:T(8,128)(2,1)S(1)} %all_to_all.22.slots_ref, bf16[384,1152]{1,0:T(8,128)(2,1)S(1)} %get-tuple-element.18.middle_ref, f32[384,128]{1,0:T(8,128)S(1)} %get-tuple-element.15.live_ref, bf16[576,1152]{1,0:T(8,128)(2,1)S(1)} %copy-done.2), custom_call_target="tpu_custom_call" | custom-call | tf_op jit(solution)/shard_map/finish/pallas_call | solution.py:432
  (5 shorter events, 0.0 us)
Async XLA Ops:
  5.8 7.8 %copy-start = (bf16[1,6,64,1152]{3,2,1,0:T(8,128)(2,1)S(1)}, bf16[1,6,64,1152]{3,2,1,0:T(8,128)(2,1)}, u32[]{:S(2)}) copy-start(bf16[1,6,64,1152]{3,2,1,0:T(8,128)(2,1)} %tokens_ref.1) | copy-start | bytes 2654212
  5.8 7.8 %copy-start.5 = (s32[1,6,8,8]{3,2,1,0:T(8,128)S(1)}, s32[1,6,8,8]{3,2,1,0:T(8,128)}, u32[]{:S(2)}) copy-start(s32[1,6,8,8]{3,2,1,0:T(8,128)} %mask_ref.1) | copy-start | bytes 4612
  5.8 7.8 %copy-start.7 = (s32[1,6]{1,0:T(1,128)S(1)}, s32[1,6]{1,0:T(1,128)}, u32[]{:S(2)}) copy-start(s32[1,6]{1,0:T(1,128)} %right_hbm.3) | copy-start | bytes 76
  5.8 7.8 %copy-start.8 = (s32[1,6]{1,0:T(1,128)S(1)}, s32[1,6]{1,0:T(1,128)}, u32[]{:S(2)}) copy-start(s32[1,6]{1,0:T(1,128)} %lengths_ref.1) | copy-start | bytes 76
  5.8 35.6 %all-to-all-start = ((bf16[16,328,128]{2,1,0:T(8,128)(2,1)}), bf16[16,328,128]{2,1,0:T(8,128)(2,1)S(1)}, u32[]{:S(2)}, u32[]{:S(2)}) async-start(bf16[16,328,128]{2,1,0:T(8,128)(2,1)} %project.1._), calls=%async_computation | async-start | bytes 2686976 | tf_op jit(solution)/shard_map/all_to_all | solution.py:444
  14.9 0.6 copy-start.3
  41.4 21.2 %copy-start.1 = (bf16[576,1152]{1,0:T(8,128)(2,1)S(1)}, bf16[576,1152]{1,0:T(8,128)(2,1)}, u32[]{:S(2)}) copy-start(bf16[576,1152]{1,0:T(8,128)(2,1)} %mix_ref.2) | copy-start | bytes 3981316
  41.4 21.2 %copy-start.6 = (f32[1152]{0:T(1024)S(1)}, f32[1152]{0:T(1024)}, u32[]{:S(2)}) copy-start(f32[1152]{0:T(1024)} %gain_ref.1) | copy-start | bytes 13828
  68.2 35.7 %copy-start.4 = (f32[3,8,1024]{2,1,0:T(8,128)S(1)}, f32[3,8,1024]{2,1,0:T(8,128)}, u32[]{:S(2)}) copy-start(f32[3,8,1024]{2,1,0:T(8,128)} %copy-done.3) | copy-start | bytes 294916
  104.0 23.5 %copy-start.2 = (bf16[576,1152]{1,0:T(8,128)(2,1)S(1)}, bf16[576,1152]{1,0:T(8,128)(2,1)}, u32[]{:S(2)}) copy-start(bf16[576,1152]{1,0:T(8,128)(2,1)} %mix_ref.3) | copy-start | bytes 3981316

commit v6 on v5

--- a/solution.py
+++ b/solution.py
@@ -18,7 +18,7 @@
 QKV_ROWS = 328
 OUT_ROWS = 112
 NEG = -1e30
-ORDER = (9, 1, 5, 12, 0, 2, 7, 8, 14, 6, 4, 3, 15, 11, 10, 13)
+ORDER = (9, 11, 12, 15, 5, 8, 6, 1, 10, 3, 4, 14, 7, 0, 13, 2)
 PLACE = tuple(ORDER.index(device) for device in range(len(ORDER)))
 FACTOR = HS**-0.5 * 1.4426950408889634
 FIRST_GROUPS = (2, 4, 2)

time: 131 us -> 129 us (0.985)
    all_to_all x3, blocking collectives: 69.4 us -> 68.1 us  [exchange(): lax.all_to_all(slots, 'sp', split_axis=0, concat_axis=0, tiled=True, axis...]
where the time goes in v6:
time: 129 us
  blocking collectives  68.1 us (53%)
  Pallas kernels  26.1 us (20%)
  waiting for transfers between devices  25.8 us (20%)
  starting transfers between devices  7.76 us (6%)
    all_to_all x3, blocking collectives, exchange(): lax.all_to_all(slots, 'sp', split_axis=0, concat_axis=0, tiled=True, axis...  68.1 us
    pallas_call x6, Pallas kernels, call(): pl.pallas_call(kernel, out_shape=out_shape, in_specs=in_specs, out_specs=...  26.1 us
    all_to_all x1, waiting for transfers between devices, exchange(): lax.all_to_all(slots, 'sp', split_axis=0, concat_axis=0, tiled=True, axis...  25.8 us
    all_to_all x1, starting transfers between devices, exchange(): lax.all_to_all(slots, 'sp', split_axis=0, concat_axis=0, tiled=True, axis...  7.76 us
  transfers between devices with their start and end apart: 1, of which 1 were waited for; matrix products, arithmetic and copies ran while one was open for 0% of the time, Pallas kernels for 1%

profile of v6, /device:TPU:0, one launch (start us, length us, event | category | flops | bytes accessed | tf_op | source)
XLA Modules:
  0.0 128.7 jit_solution(18212106835045904600)
XLA Ops:
  0.0 5.7 %project.1._ = bf16[16,328,128]{2,1,0:T(8,128)(2,1)} custom-call(s32[1,6]{1,0:T(1,128)} %right_hbm.3, bf16[1,6,64,1152]{3,2,1,0:T(8,128)(2,1)} %tokens_ref.1, f32[1152]{0:T(1024)} %gain_hbm.1, bf16[1728,1152]{1,0:T(8,128)(2,1)} %bitcast.3), custom_call_target="tpu_custom_call" | custom-call | tf_op jit(solution)/shard_map/project/pallas_call | solution.py:432
  5.7 0.0 copy-start
  5.7 0.0 copy-start.5
  5.8 0.0 copy-start.7
  5.8 0.0 copy-start.8
  5.8 7.8 %all-to-all-start = ((bf16[16,328,128]{2,1,0:T(8,128)(2,1)}), bf16[16,328,128]{2,1,0:T(8,128)(2,1)S(1)}, u32[]{:S(2)}, u32[]{:S(2)}) async-start(bf16[16,328,128]{2,1,0:T(8,128)(2,1)} %project.1._), calls=%async_computation | async-start | bytes 2686976 | tf_op jit(solution)/shard_map/all_to_all | solution.py:444
  13.5 0.0 copy-done
  13.6 0.0 copy-done.5
  13.6 0.0 copy-done.7
  13.6 0.0 copy-done.8
  13.6 1.3 prepare.1
  14.8 0.0 copy-start.3
  14.9 0.6 copy-done.3
  15.5 25.8 %all-to-all-done.slots_ref = bf16[16,328,128]{2,1,0:T(8,128)(2,1)S(1)} async-done(((bf16[16,328,128]{2,1,0:T(8,128)(2,1)}), bf16[16,328,128]{2,1,0:T(8,128)(2,1)S(1)}, u32[]{:S(2)}, u32[]{:S(2)}) %all-to-all-start) | async-done | bytes 1343520 | tf_op jit(solution)/shard_map/all_to_all | solution.py:444
  41.3 3.2 %spatial.1 = bf16[16,112,128]{2,1,0:T(8,128)(2,1)S(1)} custom-call(bf16[16,328,128]{2,1,0:T(8,128)(2,1)S(1)} %all-to-all-done.slots_ref, f32[3,8,1024]{2,1,0:T(8,128)S(1)} %get-tuple-element.12.rows_ref, f32[3,8,1024]{2,1,0:T(8,128)S(1)} %get-tuple-element.13.bias_ref), custom_call_target="tpu_custom_call" | custom-call | tf_op jit(solution)/shard_map/spatial/pallas_call | solution.py:432
  44.6 17.6 %all_to_all.20.slots_ref = bf16[16,112,128]{2,1,0:T(8,128)(2,1)S(1)} all-to-all(bf16[16,112,128]{2,1,0:T(8,128)(2,1)S(1)} %spatial.1), channel_id=1, replica_groups={{9,11,12,15,5,8,6,1,10,3,4,14,7,0,13,2},{25,27,28,31,21,24,22,17,26,19,..., dimensions={0} | all-to-all | bytes 917504 | tf_op jit(solution)/shard_map/all_to_all | solution.py:444
  62.2 0.0 copy-done.6
  62.2 5.6 %middle.1 = (bf16[384,1152]{1,0:T(8,128)(2,1)S(1)}, bf16[16,328,128]{2,1,0:T(8,128)(2,1)S(1)}) custom-call(bf16[16,112,128]{2,1,0:T(8,128)(2,1)S(1)} %all_to_all.20.slots_ref, bf16[384,1152]{1,0:T(8,128)(2,1)S(1)} %get-tuple-element.14.tokens_ref, f32[384,128]{1,0:T(8,128)S(1)} %get-tuple-element.15.live_ref, bf16[576,1152]{1,0:T(8,128)(2,1)S(1)} %copy-done.1, ...), custom_call_target="tpu_custom_call" | custom-call | tf_op jit(solution)/shard_map/middle/pallas_call | solution.py:432
  67.8 0.0 copy-start.4
  67.8 35.3 %all_to_all.21.slots_ref = bf16[16,328,128]{2,1,0:T(8,128)(2,1)S(1)} all-to-all(bf16[16,328,128]{2,1,0:T(8,128)(2,1)S(1)} %get-tuple-element.16), channel_id=1, replica_groups={{9,11,12,15,5,8,6,1,10,3,4,14,7,0,13,2},{25,27,28,31,21,24,22,17,26,19,..., dimensions={0} | all-to-all | bytes 2686976 | tf_op jit(solution)/shard_map/all_to_all | solution.py:444
  103.1 0.0 copy-done.4
  103.1 7.7 %cross.1 = bf16[16,112,128]{2,1,0:T(8,128)(2,1)S(1)} custom-call(bf16[16,328,128]{2,1,0:T(8,128)(2,1)S(1)} %all_to_all.21.slots_ref, f32[3,8,1024]{2,1,0:T(8,128)S(1)} %copy-done.4), custom_call_target="tpu_custom_call" | custom-call | tf_op jit(solution)/shard_map/cross/pallas_call | solution.py:432
  110.9 15.1 %all_to_all.22.slots_ref = bf16[16,112,128]{2,1,0:T(8,128)(2,1)S(1)} all-to-all(bf16[16,112,128]{2,1,0:T(8,128)(2,1)S(1)} %cross.1), channel_id=1, replica_groups={{9,11,12,15,5,8,6,1,10,3,4,14,7,0,13,2},{25,27,28,31,21,24,22,17,26,19,..., dimensions={0} | all-to-all | bytes 917504 | tf_op jit(solution)/shard_map/all_to_all | solution.py:444
  126.0 2.6 %finish.1 = bf16[1,6,64,1152]{3,2,1,0:T(8,128)(2,1)} custom-call(s32[1,6]{1,0:T(1,128)} %right_hbm.3, bf16[16,112,128]{2,1,0:T(8,128)(2,1)S(1)} %all_to_all.22.slots_ref, bf16[384,1152]{1,0:T(8,128)(2,1)S(1)} %get-tuple-element.18.middle_ref, f32[384,128]{1,0:T(8,128)S(1)} %get-tuple-element.15.live_ref, bf16[576,1152]{1,0:T(8,128)(2,1)S(1)} %copy-done.2), custom_call_target="tpu_custom_call" | custom-call | tf_op jit(solution)/shard_map/finish/pallas_call | solution.py:432
  (5 shorter events, 0.0 us)
Async XLA Ops:
  5.7 7.8 %copy-start = (bf16[1,6,64,1152]{3,2,1,0:T(8,128)(2,1)S(1)}, bf16[1,6,64,1152]{3,2,1,0:T(8,128)(2,1)}, u32[]{:S(2)}) copy-start(bf16[1,6,64,1152]{3,2,1,0:T(8,128)(2,1)} %tokens_ref.1) | copy-start | bytes 2654212
  5.7 7.8 %copy-start.5 = (s32[1,6,8,8]{3,2,1,0:T(8,128)S(1)}, s32[1,6,8,8]{3,2,1,0:T(8,128)}, u32[]{:S(2)}) copy-start(s32[1,6,8,8]{3,2,1,0:T(8,128)} %mask_ref.1) | copy-start | bytes 4612
  5.8 7.8 %copy-start.7 = (s32[1,6]{1,0:T(1,128)S(1)}, s32[1,6]{1,0:T(1,128)}, u32[]{:S(2)}) copy-start(s32[1,6]{1,0:T(1,128)} %right_hbm.3) | copy-start | bytes 76
  5.8 7.8 %copy-start.8 = (s32[1,6]{1,0:T(1,128)S(1)}, s32[1,6]{1,0:T(1,128)}, u32[]{:S(2)}) copy-start(s32[1,6]{1,0:T(1,128)} %lengths_ref.1) | copy-start | bytes 76
  5.8 35.5 %all-to-all-start = ((bf16[16,328,128]{2,1,0:T(8,128)(2,1)}), bf16[16,328,128]{2,1,0:T(8,128)(2,1)S(1)}, u32[]{:S(2)}, u32[]{:S(2)}) async-start(bf16[16,328,128]{2,1,0:T(8,128)(2,1)} %project.1._), calls=%async_computation | async-start | bytes 2686976 | tf_op jit(solution)/shard_map/all_to_all | solution.py:444
  14.8 0.6 copy-start.3
  41.3 20.9 %copy-start.1 = (bf16[576,1152]{1,0:T(8,128)(2,1)S(1)}, bf16[576,1152]{1,0:T(8,128)(2,1)}, u32[]{:S(2)}) copy-start(bf16[576,1152]{1,0:T(8,128)(2,1)} %mix_ref.2) | copy-start | bytes 3981316
  41.3 20.9 %copy-start.6 = (f32[1152]{0:T(1024)S(1)}, f32[1152]{0:T(1024)}, u32[]{:S(2)}) copy-start(f32[1152]{0:T(1024)} %gain_ref.1) | copy-start | bytes 13828
  67.8 35.3 %copy-start.4 = (f32[3,8,1024]{2,1,0:T(8,128)S(1)}, f32[3,8,1024]{2,1,0:T(8,128)}, u32[]{:S(2)}) copy-start(f32[3,8,1024]{2,1,0:T(8,128)} %copy-done.3) | copy-start | bytes 294916
  103.1 22.9 %copy-start.2 = (bf16[576,1152]{1,0:T(8,128)(2,1)S(1)}, bf16[576,1152]{1,0:T(8,128)(2,1)}, u32[]{:S(2)}) copy-start(bf16[576,1152]{1,0:T(8,128)(2,1)} %mix_ref.3) | copy-start | bytes 3981316

commit v7 on v6

--- a/solution.py
+++ b/solution.py
@@ -15,7 +15,7 @@
 TILE = 64
 LANES = 128
 TOP = 40
-QKV_ROWS = 328
+QKV_ROWS = 336
 OUT_ROWS = 112
 NEG = -1e30
 ORDER = (9, 11, 12, 15, 5, 8, 6, 1, 10, 3, 4, 14, 7, 0, 13, 2)
@@ -83,6 +83,7 @@
                 ]
                 rows.append(side_by_side(item(2, views[0]), other, item(2, views[1]), other))
                 rows.append(fold_third(item(2, views[2]), other))
+                rows.append(jnp.zeros((QKV_ROWS - 4 * HS - TOP, LANES), jnp.float32))
                 slot = PLACE[(head + inside) * 2 + parity]
                 slots_ref[slot] = jnp.concatenate(rows, axis=0).astype(jnp.bfloat16)
 

time: 129 us -> 131 us (1.016)
  no operation moved by 1% of the time
where the time goes in v7:
time: 131 us; the launch traced here: 130 us
  blocking collectives  68.8 us (53%)
  Pallas kernels  26.1 us (20%)
  waiting for transfers between devices  25.8 us (20%)
  starting transfers between devices  7.76 us (6%)
  local copies, waits for them, and re-layouts  1.4 us (1%)
    all_to_all x3, blocking collectives, exchange(): lax.all_to_all(slots, 'sp', split_axis=0, concat_axis=0, tiled=True, axis...  68.8 us
    pallas_call x6, Pallas kernels, call(): pl.pallas_call(kernel, out_shape=out_shape, in_specs=in_specs, out_specs=...  26.1 us
    all_to_all x1, waiting for transfers between devices, exchange(): lax.all_to_all(slots, 'sp', split_axis=0, concat_axis=0, tiled=True, axis...  25.8 us
    all_to_all x1, starting transfers between devices, exchange(): lax.all_to_all(slots, 'sp', split_axis=0, concat_axis=0, tiled=True, axis...  7.76 us
  transfers between devices with their start and end apart: 1, of which 1 were waited for; matrix products, arithmetic and copies ran while one was open for 0% of the time, Pallas kernels for 1%

profile of v7, /device:TPU:0, one launch (start us, length us, event | category | flops | bytes accessed | tf_op | source)
XLA Modules:
  0.0 130.1 jit_solution(5381521830866652381)
XLA Ops:
  0.0 5.7 %project.1._ = bf16[16,336,128]{2,1,0:T(8,128)(2,1)} custom-call(s32[1,6]{1,0:T(1,128)} %right_hbm.3, bf16[1,6,64,1152]{3,2,1,0:T(8,128)(2,1)} %tokens_ref.1, f32[1152]{0:T(1024)} %gain_hbm.1, bf16[1728,1152]{1,0:T(8,128)(2,1)} %bitcast.3), custom_call_target="tpu_custom_call" | custom-call | tf_op jit(solution)/shard_map/project/pallas_call | solution.py:433
  5.7 0.0 copy-start
  5.7 0.0 copy-start.7
  5.8 0.0 copy-start.8
  5.8 7.8 %all-to-all-start = ((bf16[16,336,128]{2,1,0:T(8,128)(2,1)}), bf16[16,336,128]{2,1,0:T(8,128)(2,1)S(1)}, u32[]{:S(2)}, u32[]{:S(2)}) async-start(bf16[16,336,128]{2,1,0:T(8,128)(2,1)} %project.1._), calls=%async_computation | async-start | bytes 2752512 | tf_op jit(solution)/shard_map/all_to_all | solution.py:445
  13.5 0.0 copy-done
  13.5 0.0 copy-done.7
  13.5 0.0 copy-done.8
  13.6 0.0 copy-start.5
  13.6 0.7 copy-done.5
  14.3 1.3 prepare.1
  15.6 0.0 copy-start.3
  15.6 0.6 copy-done.3
  16.2 25.8 %all-to-all-done.slots_ref = bf16[16,336,128]{2,1,0:T(8,128)(2,1)S(1)} async-done(((bf16[16,336,128]{2,1,0:T(8,128)(2,1)}), bf16[16,336,128]{2,1,0:T(8,128)(2,1)S(1)}, u32[]{:S(2)}, u32[]{:S(2)}) %all-to-all-start) | async-done | bytes 1376288 | tf_op jit(solution)/shard_map/all_to_all | solution.py:445
  42.0 3.2 %spatial.1 = bf16[16,112,128]{2,1,0:T(8,128)(2,1)S(1)} custom-call(bf16[16,336,128]{2,1,0:T(8,128)(2,1)S(1)} %all-to-all-done.slots_ref, f32[3,8,1024]{2,1,0:T(8,128)S(1)} %get-tuple-element.12.rows_ref, f32[3,8,1024]{2,1,0:T(8,128)S(1)} %get-tuple-element.13.bias_ref), custom_call_target="tpu_custom_call" | custom-call | tf_op jit(solution)/shard_map/spatial/pallas_call | solution.py:433
  45.2 17.7 %all_to_all.20.slots_ref = bf16[16,112,128]{2,1,0:T(8,128)(2,1)S(1)} all-to-all(bf16[16,112,128]{2,1,0:T(8,128)(2,1)S(1)} %spatial.1), channel_id=1, replica_groups={{9,11,12,15,5,8,6,1,10,3,4,14,7,0,13,2},{25,27,28,31,21,24,22,17,26,19,..., dimensions={0} | all-to-all | bytes 917504 | tf_op jit(solution)/shard_map/all_to_all | solution.py:445
  62.9 0.0 copy-done.1
  62.9 0.0 copy-done.6
  62.9 5.6 %middle.1 = (bf16[384,1152]{1,0:T(8,128)(2,1)S(1)}, bf16[16,336,128]{2,1,0:T(8,128)(2,1)S(1)}) custom-call(bf16[16,112,128]{2,1,0:T(8,128)(2,1)S(1)} %all_to_all.20.slots_ref, bf16[384,1152]{1,0:T(8,128)(2,1)S(1)} %get-tuple-element.14.tokens_ref, f32[384,128]{1,0:T(8,128)S(1)} %get-tuple-element.15.live_ref, bf16[576,1152]{1,0:T(8,128)(2,1)S(1)} %copy-done.1, ...), custom_call_target="tpu_custom_call" | custom-call | tf_op jit(solution)/shard_map/middle/pallas_call | solution.py:433
  68.5 0.0 copy-start.4
  68.5 35.9 %all_to_all.21.slots_ref = bf16[16,336,128]{2,1,0:T(8,128)(2,1)S(1)} all-to-all(bf16[16,336,128]{2,1,0:T(8,128)(2,1)S(1)} %get-tuple-element.16), channel_id=1, replica_groups={{9,11,12,15,5,8,6,1,10,3,4,14,7,0,13,2},{25,27,28,31,21,24,22,17,26,19,..., dimensions={0} | all-to-all | bytes 2752512 | tf_op jit(solution)/shard_map/all_to_all | solution.py:445
  104.4 7.7 %cross.1 = bf16[16,112,128]{2,1,0:T(8,128)(2,1)S(1)} custom-call(bf16[16,336,128]{2,1,0:T(8,128)(2,1)S(1)} %all_to_all.21.slots_ref, f32[3,8,1024]{2,1,0:T(8,128)S(1)} %copy-done.4), custom_call_target="tpu_custom_call" | custom-call | tf_op jit(solution)/shard_map/cross/pallas_call | solution.py:433
  112.1 15.2 %all_to_all.22.slots_ref = bf16[16,112,128]{2,1,0:T(8,128)(2,1)S(1)} all-to-all(bf16[16,112,128]{2,1,0:T(8,128)(2,1)S(1)} %cross.1), channel_id=1, replica_groups={{9,11,12,15,5,8,6,1,10,3,4,14,7,0,13,2},{25,27,28,31,21,24,22,17,26,19,..., dimensions={0} | all-to-all | bytes 917504 | tf_op jit(solution)/shard_map/all_to_all | solution.py:445
  127.3 2.6 %finish.1 = bf16[1,6,64,1152]{3,2,1,0:T(8,128)(2,1)} custom-call(s32[1,6]{1,0:T(1,128)} %right_hbm.3, bf16[16,112,128]{2,1,0:T(8,128)(2,1)S(1)} %all_to_all.22.slots_ref, bf16[384,1152]{1,0:T(8,128)(2,1)S(1)} %get-tuple-element.18.middle_ref, f32[384,128]{1,0:T(8,128)S(1)} %get-tuple-element.15.live_ref, bf16[576,1152]{1,0:T(8,128)(2,1)S(1)} %copy-done.2), custom_call_target="tpu_custom_call" | custom-call | tf_op jit(solution)/shard_map/finish/pallas_call | solution.py:433
  (5 shorter events, 0.0 us)
Async XLA Ops:
  5.7 7.8 %copy-start = (bf16[1,6,64,1152]{3,2,1,0:T(8,128)(2,1)S(1)}, bf16[1,6,64,1152]{3,2,1,0:T(8,128)(2,1)}, u32[]{:S(2)}) copy-start(bf16[1,6,64,1152]{3,2,1,0:T(8,128)(2,1)} %tokens_ref.1) | copy-start | bytes 2654212
  5.7 7.8 %copy-start.7 = (s32[1,6]{1,0:T(1,128)S(1)}, s32[1,6]{1,0:T(1,128)}, u32[]{:S(2)}) copy-start(s32[1,6]{1,0:T(1,128)} %right_hbm.3) | copy-start | bytes 76
  5.8 7.8 %copy-start.8 = (s32[1,6]{1,0:T(1,128)S(1)}, s32[1,6]{1,0:T(1,128)}, u32[]{:S(2)}) copy-start(s32[1,6]{1,0:T(1,128)} %lengths_ref.1) | copy-start | bytes 76
  5.8 36.2 %all-to-all-start = ((bf16[16,336,128]{2,1,0:T(8,128)(2,1)}), bf16[16,336,128]{2,1,0:T(8,128)(2,1)S(1)}, u32[]{:S(2)}, u32[]{:S(2)}) async-start(bf16[16,336,128]{2,1,0:T(8,128)(2,1)} %project.1._), calls=%async_computation | async-start | bytes 2752512 | tf_op jit(solution)/shard_map/all_to_all | solution.py:445
  13.6 0.7 copy-start.5
  15.6 0.6 copy-start.3
  42.0 20.9 %copy-start.1 = (bf16[576,1152]{1,0:T(8,128)(2,1)S(1)}, bf16[576,1152]{1,0:T(8,128)(2,1)}, u32[]{:S(2)}) copy-start(bf16[576,1152]{1,0:T(8,128)(2,1)} %mix_ref.2) | copy-start | bytes 3981316
  42.0 20.9 %copy-start.6 = (f32[1152]{0:T(1024)S(1)}, f32[1152]{0:T(1024)}, u32[]{:S(2)}) copy-start(f32[1152]{0:T(1024)} %gain_ref.1) | copy-start | bytes 13828
  68.5 35.9 %copy-start.4 = (f32[3,8,1024]{2,1,0:T(8,128)S(1)}, f32[3,8,1024]{2,1,0:T(8,128)}, u32[]{:S(2)}) copy-start(f32[3,8,1024]{2,1,0:T(8,128)} %copy-done.3) | copy-start | bytes 294916
  104.4 22.9 %copy-start.2 = (bf16[576,1152]{1,0:T(8,128)(2,1)S(1)}, bf16[576,1152]{1,0:T(8,128)(2,1)}, u32[]{:S(2)}) copy-start(bf16[576,1152]{1,0:T(8,128)(2,1)} %mix_ref.3) | copy-start | bytes 3981316

commit v8 on v7

--- a/solution.py
+++ b/solution.py
@@ -271,7 +271,7 @@
             )
 
 
-def attend(jobs, query_ref, key_ref, value_ref, attended_ref):
+def attend(jobs, query_ref, key_ref, value_ref, attended_ref, depth):
     def scores(job):
         m, lanes, parts = job
         query = query_ref[m, :, lanes]
@@ -295,7 +295,7 @@
     queue = []
     for job in jobs:
         queue.append((job, scores(job)))
-        if len(queue) > 2:
+        if len(queue) > depth:
             finish(*queue.pop(0))
     for entry in queue:
         finish(*entry)
@@ -325,7 +325,7 @@
             if first > 0:
                 spans.append(slice(0, LANES))
             jobs.append((m, slice(i * wide, (i + 1) * wide), [(m, span) for span in spans]))
-    attend(jobs, query_ref, key_ref, value_ref, attended_ref)
+    attend(jobs, query_ref, key_ref, value_ref, attended_ref, 3)
     pack_outputs(attended_ref, out_ref)
 
 
@@ -338,7 +338,7 @@
         second = (m + 1) % 3
         for i in range(query_ref.shape[2] // wide):
             jobs.append((m, slice(i * wide, (i + 1) * wide), [(m, every), (second, every)]))
-    attend(jobs, query_ref, key_ref, value_ref, attended_ref)
+    attend(jobs, query_ref, key_ref, value_ref, attended_ref, 2)
     pack_outputs(attended_ref, out_ref)
 
 

time: 131 us -> 131 us (level)
  no operation moved by 1% of the time
where the time goes in v8:
time: 131 us; the launch traced here: 130 us
  blocking collectives  68.8 us (53%)
  Pallas kernels  26 us (20%)
  waiting for transfers between devices  25.8 us (20%)
  starting transfers between devices  7.76 us (6%)
  local copies, waits for them, and re-layouts  1.4 us (1%)
    all_to_all x3, blocking collectives, exchange(): lax.all_to_all(slots, 'sp', split_axis=0, concat_axis=0, tiled=True, axis...  68.8 us
    pallas_call x6, Pallas kernels, call(): pl.pallas_call(kernel, out_shape=out_shape, in_specs=in_specs, out_specs=...  26 us
    all_to_all x1, waiting for transfers between devices, exchange(): lax.all_to_all(slots, 'sp', split_axis=0, concat_axis=0, tiled=True, axis...  25.8 us
    all_to_all x1, starting transfers between devices, exchange(): lax.all_to_all(slots, 'sp', split_axis=0, concat_axis=0, tiled=True, axis...  7.76 us
  transfers between devices with their start and end apart: 1, of which 1 were waited for; matrix products, arithmetic and copies ran while one was open for 0% of the time, Pallas kernels for 1%

profile of v8, /device:TPU:0, one launch (start us, length us, event | category | flops | bytes accessed | tf_op | source)
XLA Modules:
  0.0 129.9 jit_solution(4600603462298872537)
XLA Ops:
  0.0 5.7 %project.1._ = bf16[16,336,128]{2,1,0:T(8,128)(2,1)} custom-call(s32[1,6]{1,0:T(1,128)} %right_hbm.3, bf16[1,6,64,1152]{3,2,1,0:T(8,128)(2,1)} %tokens_ref.1, f32[1152]{0:T(1024)} %gain_hbm.1, bf16[1728,1152]{1,0:T(8,128)(2,1)} %bitcast.3), custom_call_target="tpu_custom_call" | custom-call | tf_op jit(solution)/shard_map/project/pallas_call | solution.py:433
  5.7 0.0 copy-start
  5.7 0.0 copy-start.7
  5.8 0.0 copy-start.8
  5.8 7.8 %all-to-all-start = ((bf16[16,336,128]{2,1,0:T(8,128)(2,1)}), bf16[16,336,128]{2,1,0:T(8,128)(2,1)S(1)}, u32[]{:S(2)}, u32[]{:S(2)}) async-start(bf16[16,336,128]{2,1,0:T(8,128)(2,1)} %project.1._), calls=%async_computation | async-start | bytes 2752512 | tf_op jit(solution)/shard_map/all_to_all | solution.py:445
  13.5 0.0 copy-done
  13.5 0.0 copy-done.7
  13.5 0.0 copy-done.8
  13.6 0.0 copy-start.5
  13.6 0.7 copy-done.5
  14.3 1.3 prepare.1
  15.6 0.0 copy-start.3
  15.6 0.6 copy-done.3
  16.2 25.8 %all-to-all-done.slots_ref = bf16[16,336,128]{2,1,0:T(8,128)(2,1)S(1)} async-done(((bf16[16,336,128]{2,1,0:T(8,128)(2,1)}), bf16[16,336,128]{2,1,0:T(8,128)(2,1)S(1)}, u32[]{:S(2)}, u32[]{:S(2)}) %all-to-all-start) | async-done | bytes 1376288 | tf_op jit(solution)/shard_map/all_to_all | solution.py:445
  42.0 3.1 %spatial.1 = bf16[16,112,128]{2,1,0:T(8,128)(2,1)S(1)} custom-call(bf16[16,336,128]{2,1,0:T(8,128)(2,1)S(1)} %all-to-all-done.slots_ref, f32[3,8,1024]{2,1,0:T(8,128)S(1)} %get-tuple-element.12.rows_ref, f32[3,8,1024]{2,1,0:T(8,128)S(1)} %get-tuple-element.13.bias_ref), custom_call_target="tpu_custom_call" | custom-call | tf_op jit(solution)/shard_map/spatial/pallas_call | solution.py:433
  45.1 17.7 %all_to_all.20.slots_ref = bf16[16,112,128]{2,1,0:T(8,128)(2,1)S(1)} all-to-all(bf16[16,112,128]{2,1,0:T(8,128)(2,1)S(1)} %spatial.1), channel_id=1, replica_groups={{9,11,12,15,5,8,6,1,10,3,4,14,7,0,13,2},{25,27,28,31,21,24,22,17,26,19,..., dimensions={0} | all-to-all | bytes 917504 | tf_op jit(solution)/shard_map/all_to_all | solution.py:445
  62.8 0.0 copy-done.6
  62.8 5.6 %middle.1 = (bf16[384,1152]{1,0:T(8,128)(2,1)S(1)}, bf16[16,336,128]{2,1,0:T(8,128)(2,1)S(1)}) custom-call(bf16[16,112,128]{2,1,0:T(8,128)(2,1)S(1)} %all_to_all.20.slots_ref, bf16[384,1152]{1,0:T(8,128)(2,1)S(1)} %get-tuple-element.14.tokens_ref, f32[384,128]{1,0:T(8,128)S(1)} %get-tuple-element.15.live_ref, bf16[576,1152]{1,0:T(8,128)(2,1)S(1)} %copy-done.1, ...), custom_call_target="tpu_custom_call" | custom-call | tf_op jit(solution)/shard_map/middle/pallas_call | solution.py:433
  68.4 0.0 copy-start.4
  68.4 35.9 %all_to_all.21.slots_ref = bf16[16,336,128]{2,1,0:T(8,128)(2,1)S(1)} all-to-all(bf16[16,336,128]{2,1,0:T(8,128)(2,1)S(1)} %get-tuple-element.16), channel_id=1, replica_groups={{9,11,12,15,5,8,6,1,10,3,4,14,7,0,13,2},{25,27,28,31,21,24,22,17,26,19,..., dimensions={0} | all-to-all | bytes 2752512 | tf_op jit(solution)/shard_map/all_to_all | solution.py:445
  104.3 0.0 copy-done.4
  104.3 7.7 %cross.1 = bf16[16,112,128]{2,1,0:T(8,128)(2,1)S(1)} custom-call(bf16[16,336,128]{2,1,0:T(8,128)(2,1)S(1)} %all_to_all.21.slots_ref, f32[3,8,1024]{2,1,0:T(8,128)S(1)} %copy-done.4), custom_call_target="tpu_custom_call" | custom-call | tf_op jit(solution)/shard_map/cross/pallas_call | solution.py:433
  112.0 15.2 %all_to_all.22.slots_ref = bf16[16,112,128]{2,1,0:T(8,128)(2,1)S(1)} all-to-all(bf16[16,112,128]{2,1,0:T(8,128)(2,1)S(1)} %cross.1), channel_id=1, replica_groups={{9,11,12,15,5,8,6,1,10,3,4,14,7,0,13,2},{25,27,28,31,21,24,22,17,26,19,..., dimensions={0} | all-to-all | bytes 917504 | tf_op jit(solution)/shard_map/all_to_all | solution.py:445
  127.2 2.6 %finish.1 = bf16[1,6,64,1152]{3,2,1,0:T(8,128)(2,1)} custom-call(s32[1,6]{1,0:T(1,128)} %right_hbm.3, bf16[16,112,128]{2,1,0:T(8,128)(2,1)S(1)} %all_to_all.22.slots_ref, bf16[384,1152]{1,0:T(8,128)(2,1)S(1)} %get-tuple-element.18.middle_ref, f32[384,128]{1,0:T(8,128)S(1)} %get-tuple-element.15.live_ref, bf16[576,1152]{1,0:T(8,128)(2,1)S(1)} %copy-done.2), custom_call_target="tpu_custom_call" | custom-call | tf_op jit(solution)/shard_map/finish/pallas_call | solution.py:433
  (5 shorter events, 0.0 us)
Async XLA Ops:
  5.7 7.8 %copy-start = (bf16[1,6,64,1152]{3,2,1,0:T(8,128)(2,1)S(1)}, bf16[1,6,64,1152]{3,2,1,0:T(8,128)(2,1)}, u32[]{:S(2)}) copy-start(bf16[1,6,64,1152]{3,2,1,0:T(8,128)(2,1)} %tokens_ref.1) | copy-start | bytes 2654212
  5.7 7.8 %copy-start.7 = (s32[1,6]{1,0:T(1,128)S(1)}, s32[1,6]{1,0:T(1,128)}, u32[]{:S(2)}) copy-start(s32[1,6]{1,0:T(1,128)} %right_hbm.3) | copy-start | bytes 76
  5.8 7.8 %copy-start.8 = (s32[1,6]{1,0:T(1,128)S(1)}, s32[1,6]{1,0:T(1,128)}, u32[]{:S(2)}) copy-start(s32[1,6]{1,0:T(1,128)} %lengths_ref.1) | copy-start | bytes 76
  5.8 36.2 %all-to-all-start = ((bf16[16,336,128]{2,1,0:T(8,128)(2,1)}), bf16[16,336,128]{2,1,0:T(8,128)(2,1)S(1)}, u32[]{:S(2)}, u32[]{:S(2)}) async-start(bf16[16,336,128]{2,1,0:T(8,128)(2,1)} %project.1._), calls=%async_computation | async-start | bytes 2752512 | tf_op jit(solution)/shard_map/all_to_all | solution.py:445
  13.6 0.7 copy-start.5
  15.6 0.6 copy-start.3
  42.0 20.8 %copy-start.1 = (bf16[576,1152]{1,0:T(8,128)(2,1)S(1)}, bf16[576,1152]{1,0:T(8,128)(2,1)}, u32[]{:S(2)}) copy-start(bf16[576,1152]{1,0:T(8,128)(2,1)} %mix_ref.2) | copy-start | bytes 3981316
  42.0 20.8 %copy-start.6 = (f32[1152]{0:T(1024)S(1)}, f32[1152]{0:T(1024)}, u32[]{:S(2)}) copy-start(f32[1152]{0:T(1024)} %gain_ref.1) | copy-start | bytes 13828
  68.4 35.9 %copy-start.4 = (f32[3,8,1024]{2,1,0:T(8,128)S(1)}, f32[3,8,1024]{2,1,0:T(8,128)}, u32[]{:S(2)}) copy-start(f32[3,8,1024]{2,1,0:T(8,128)} %copy-done.3) | copy-start | bytes 294916
  104.3 22.9 %copy-start.2 = (bf16[576,1152]{1,0:T(8,128)(2,1)S(1)}, bf16[576,1152]{1,0:T(8,128)(2,1)}, u32[]{:S(2)}) copy-start(bf16[576,1152]{1,0:T(8,128)(2,1)} %mix_ref.3) | copy-start | bytes 3981316
